TPU v7x, 128 devices: a whole 4x4x4 slice. The times are simulated.
128 devices in a mesh: row: 4 (over y_lo, core), col: 32 (over x, y_hi, z).
Axes of the slice: x: 4, y: 4 (y_hi: 2, y_lo: 2; y = y_hi * 2 + y_lo), z: 4, core: 2. Of those that a mesh axis runs over, the one named last changes fastest.
Arguments:
- right_side: float32 [131072], P(('row', 'col')), may hold values from -6 to 6
- eigen_basis: bfloat16 [12288, 512], P(('row', 'col')), may hold values from -0.0546875 to 0.0546875
- tile_left: bfloat16 [12288, 4096], P('row', 'col'), may hold values from -0.4375 to 0.4375
- tile_right: bfloat16 [512, 12288], P('row', 'col'), may hold values from -1.25 to 1.25
- piece_owner: int32 [4, 4096], P('row', 'col'), may hold values from 0 to 131071
- omega_main: float32 [512, 512], replicated, may hold values from 0 to 1
- damping: float32 [512], replicated, may hold values from 0.05 to 1
- local_basis: bfloat16 [1024, 256, 256], P(('row', 'col')), may hold values from -0.375 to 0.375
- local_omega: float32 [1024, 256, 256], P(('row', 'col')), may hold values from 0 to 1
- local_left: bfloat16 [1024, 256, 256], P(('row', 'col')), may hold values from -0.75 to 0.75
- local_right: bfloat16 [1024, 256, 256], P(('row', 'col')), may hold values from -0.75 to 0.75
- local_owner: int32 [1024, 256], P(('row', 'col')), may hold values from 0 to 131071
Outputs:
- solution: float32 [131072], P(('row', 'col'))
- residual: float32 [131072], P(('row', 'col'))
All inputs are finite; a program needn't handle non-finite values.
Results may differ from a plain program's by a relative error of at most 0.00057.
Values may be sent and summed in bfloat16 or wider, within the bound.
A program may use at most 128 MiB of HBM per device.

v0:
```python
import functools

import jax
import jax.numpy as jnp
from jax import lax
from jax.sharding import Mesh
from jax.sharding import PartitionSpec as P

ITERS = 2
ROW_COL = ("row_0", "row_1", "col_0", "col_1", "col_2")
COL = ("col_0", "col_1", "col_2")
ROW = ("row_0", "row_1")


precise = lax.Precision.HIGHEST
contract = (((0,), (0,)), ((), ()))


def by_axis(array, axes):
    return functools.reduce(lax.psum, axes, array)


def laid_out(parts, dim):
    parts = jnp.moveaxis(parts, 0, dim)
    dims = parts.shape
    return parts.reshape(*dims[:dim], dims[dim] * dims[dim + 1], *dims[dim + 2 :])


def from_everyone(array, axis):
    length = lax.axis_size(axis)
    return lax.all_to_all(
        jnp.broadcast_to(array[None], (length, *array.shape)), axis, 0, 0, tiled=True
    )


def collect(array, axis, dim):
    return laid_out(from_everyone(array, axis), dim)


def sum_in_order(parts, axes, sequence):
    dims = [lax.axis_size(a) for a in axes]
    parts = parts.reshape(*dims, *parts.shape[1:])
    parts = parts.transpose(*sequence, *range(len(axes), parts.ndim))
    parts = parts.reshape(-1, *parts.shape[len(axes) :])
    for k in sequence:
        parts = lax.psum_scatter(parts, axes[k], scatter_dimension=0, tiled=True)
    return parts[0]


def in_blocks(array, dim, length):
    before, after = (array.shape[:dim], array.shape[dim + 1 :])
    return jnp.moveaxis(array.reshape(*before, length, -1, *after), dim, 0)


def summed_rows(array, axes, sequence, dim):
    length = lax.axis_size(axes)
    return sum_in_order(in_blocks(array, dim, length), axes, sequence)


def sent_and_summed(array, axis, dim):
    length = lax.axis_size(axis)
    parts = lax.all_to_all(in_blocks(array, dim, length), axis, 0, 0, tiled=True)
    return jnp.sum(parts, axis=0)


def over_copies(array, axis):
    return from_everyone(array, axis).astype(jnp.float32).sum(axis=0)


def squared_sum(vector):
    return by_axis(jnp.sum(vector * vector), ROW_COL)


def local(
    right_side,
    eigen_basis,
    tile_left,
    tile_right,
    piece_owner,
    omega_main,
    damping,
    local_basis,
    local_omega,
    local_left,
    local_right,
    local_owner,
):
    basis_rows = lax.all_gather(eigen_basis, COL, axis=0, tiled=True)
    basis_cols = collect(eigen_basis, ROW, 0)
    left_proj = lax.dot_general(
        tile_left, basis_rows, contract, preferred_element_type=jnp.float32
    ).astype(jnp.bfloat16)
    right_proj = jnp.dot(tile_right, basis_cols, preferred_element_type=jnp.float32).astype(
        jnp.bfloat16
    )
    left_pf = left_proj.astype(jnp.float32)
    right_pf = right_proj.astype(jnp.float32)
    local_lp = jnp.einsum(
        "lps,lsk->lpk", local_left, local_basis, preferred_element_type=jnp.float32
    ).astype(jnp.bfloat16)
    local_rp = jnp.einsum(
        "lps,lsk->lpk", local_right, local_basis, preferred_element_type=jnp.float32
    ).astype(jnp.bfloat16)
    left_float = local_lp.astype(jnp.float32)
    right_float = local_rp.astype(jnp.float32)
    owners = piece_owner[0]
    local_flat = local_owner.reshape(-1)
    omega_sym = 0.5 * (omega_main + omega_main.T)
    local_sym = 0.5 * (local_omega + jnp.swapaxes(local_omega, 1, 2))
    solution = jnp.zeros_like(right_side)
    residual = right_side
    direction = right_side
    norm_now = squared_sum(residual)
    for counter in range(ITERS):
        all_duals = lax.all_gather(direction, ROW_COL, axis=0, tiled=True)
        coeffs = all_duals[owners]
        scaled_right = (coeffs[:, None] * right_pf).astype(jnp.bfloat16)
        scaled_left = (coeffs[:, None] * left_pf).astype(jnp.bfloat16)
        row_terms = jnp.dot(tile_left, scaled_right, preferred_element_type=jnp.float32)
        row_share = summed_rows(row_terms, COL, (0, 2, 1), 0)
        col_terms = lax.dot_general(
            tile_right, scaled_left, contract, preferred_element_type=jnp.float32
        )
        col_share = sent_and_summed(col_terms, ROW, 0)
        field_half = (row_share + col_share).astype(jnp.bfloat16)
        field_rows = lax.all_gather(field_half, COL, axis=0, tiled=True)
        field_cols = collect(field_half, ROW, 0)
        own_terms = lax.dot_general(
            basis_rows, field_rows, contract, preferred_element_type=jnp.float32
        )
        curvature = over_copies(own_terms.astype(jnp.bfloat16), ROW).astype(jnp.float32)
        weights = omega_sym * curvature
        left_field = lax.dot_general(
            tile_left, field_rows, contract, preferred_element_type=jnp.float32
        )
        right_field = jnp.dot(tile_right, field_cols, preferred_element_type=jnp.float32)
        left_rest = left_field - jnp.dot(left_pf, curvature, precision=precise)
        right_rest = right_field - jnp.dot(right_pf, curvature, precision=precise)
        weighted = jnp.dot(right_pf, weights, precision=precise)
        inner_sum = (
            left_pf * weighted + left_rest * (damping * right_pf) + damping * left_pf * right_rest
        )
        big_values = 2.0 * jnp.sum(inner_sum, axis=1)
        local_coeffs = all_duals[local_owner]
        scaled = local_coeffs[:, :, None] * left_float
        half_t = jnp.einsum("lpa,lpb->lab", scaled, right_float, precision=precise)
        gram_mat = half_t + jnp.swapaxes(half_t, 1, 2)
        local_w = local_sym * gram_mat
        mixed_rows = jnp.einsum("lpb,lba->lpa", right_float, local_w, precision=precise)
        local_values = 2.0 * jnp.sum(left_float * mixed_rows, axis=2)
        totals = jnp.zeros((all_duals.shape[0],), jnp.float32).at[owners].add(big_values)
        totals = totals.at[local_flat].add(local_values.reshape(-1))
        returned = lax.psum_scatter(totals, ROW_COL, scatter_dimension=0, tiled=True)
        applied = direction + returned
        step_size = norm_now / by_axis(jnp.sum(direction * applied), ROW_COL)
        solution = solution + step_size * direction
        residual = residual - step_size * applied
        norm_next = squared_sum(residual)
        direction = residual + norm_next / norm_now * direction
        norm_now = norm_next
    return (solution, residual)


def solution(mesh):
    torus = Mesh(mesh.devices.reshape(2, 2, 4, 2, 4), ("row_0", "row_1", "col_0", "col_1", "col_2"))
    placed = (
        P(ROW_COL),
        P(ROW_COL, None),
        P(ROW, COL),
        P(ROW, COL),
        P(ROW, COL),
        P(),
        P(),
        P(ROW_COL, None, None),
        P(ROW_COL, None, None),
        P(ROW_COL, None, None),
        P(ROW_COL, None, None),
        P(ROW_COL, None),
    )
    return jax.shard_map(
        local, mesh=torus, in_specs=placed, out_specs=(P(ROW_COL), P(ROW_COL)), check_vma=False
    )
```

profile of v0, /device:TPU:1, one launch (start us, length us, event | category | flops | bytes accessed | tf_op | source)
XLA Modules:
  0.0 1634.1 jit_solution(9172988969197644502)
XLA Ops:
  15.3 330.9 %all_gather.16 = f32[131072]{0:T(1024)S(1)} all-gather(f32[1024]{0:T(1024)} %param.12), channel_id=1, replica_groups=mesh['row_0'=2,'row_1'=2,'col_0'=4,'col_1'=2,'col_2'=4] {'row_0','row_1'..., dimensions={0}, use_global_device_ids=true | all-gather | bytes 528384 | tf_op jit(solution)/shard_map/all_gather | solution.py:115
  351.4 6.5 copy.62
  357.9 6.6 copy.63
  365.2 58.6 %reduce-scatter.7.cloned.1.call-done = f32[8,96,512]{2,1,0:T(8,128)} async-done(((f32[32,96,512]{2,1,0:T(8,128)}), f32[8,96,512]{2,1,0:T(8,128)}) %reduce-scatter.7.cloned.1.call-update) | async-done | bytes 1572880 | tf_op jit(solution)/shard_map/reduce_scatter | solution.py:46
  423.8 53.5 %all-gather.4.cloned.1.call-done = bf16[3072,512]{1,0:T(8,128)(2,1)} async-done(((bf16[96,512]{1,0:T(8,128)(2,1)}), bf16[3072,512]{1,0:T(8,128)(2,1)}) %all-gather.4.cloned.1.call-update) | async-done | bytes 3145744 | tf_op jit(solution)/shard_map/all_gather | solution.py:88
  480.3 20.1 %all_to_all.35 = f32[4,96,512]{2,1,0:T(8,128)} all-to-all(f32[4,96,512]{2,1,0:T(8,128)S(1)} %bitcast.167), channel_id=1, replica_groups=mesh['row_0'=2,'row_1'=2,'col_0'=4,'col_1'=2,'col_2'=4] {'row_0','row_1'}, dimensions={0} | all-to-all | bytes 1572864 | tf_op jit(solution)/shard_map/all_to_all | solution.py:62
  504.7 11.8 gather_fusion.1
  527.2 47.6 %all-gather.6.cloned.1.call-done = bf16[3072,512]{1,0:T(8,128)(2,1)} async-done(((bf16[96,512]{1,0:T(8,128)(2,1)}), bf16[3072,512]{1,0:T(8,128)(2,1)}) %all-gather.6.cloned.1.call-update) | async-done | bytes 3145744 | tf_op jit(solution)/shard_map/all_gather | solution.py:126
  581.2 6.5 all-to-all-start.2
  595.4 17.3 %all-to-all-done.2 = bf16[4,512,512]{2,1,0:T(8,128)(2,1)} async-done(((bf16[4,512,512]{2,1,0:T(8,128)(2,1)}), bf16[4,512,512]{2,1,0:T(8,128)(2,1)}, u32[]{:S(2)}, u32[]{:S(2)}) %all-to-all-start.2) | async-done | bytes 2097184 | tf_op jit(solution)/shard_map/all_to_all | solution.py:31
  627.9 11.7 scatter_fusion
  640.5 142.0 %all-reduce.10.cloned.1.call-done = f32[131072]{0:T(1024)} async-done(((f32[131072]{0:T(1024)}), f32[131072]{0:T(1024)}) %all-reduce.10.cloned.1.call-update) | async-done | bytes 524304
  792.0 8.3 all-reduce.3
  800.3 5.9 all-reduce.4
  806.2 8.6 all-reduce.2
  821.8 9.4 psum.151
  831.2 6.7 psum.152
  843.8 6.6 psum.154
  852.5 331.0 %all_gather.18 = f32[131072]{0:T(1024)S(1)} all-gather(f32[1024]{0:T(1024)S(1)} %multiply_add_fusion.1), channel_id=1, replica_groups=mesh['row_0'=2,'row_1'=2,'col_0'=4,'col_1'=2,'col_2'=4] {'row_0','row_1'..., dimensions={0}, use_global_device_ids=true | all-gather | bytes 528384 | tf_op jit(solution)/shard_map/all_gather | solution.py:115
  1189.5 6.6 copy.71
  1196.1 6.6 copy.72
  1202.7 57.2 %reduce-scatter.13.cloned.1.call-done = f32[8,96,512]{2,1,0:T(8,128)} async-done(((f32[32,96,512]{2,1,0:T(8,128)}), f32[8,96,512]{2,1,0:T(8,128)}) %reduce-scatter.13.cloned.1.call-update) | async-done | bytes 1572880 | tf_op jit(solution)/shard_map/reduce_scatter | solution.py:46
  1260.0 27.0 %reduce-scatter.15.cloned.1.call-done = f32[2,96,512]{2,1,0:T(8,128)} async-done(((f32[8,96,512]{2,1,0:T(8,128)}), f32[2,96,512]{2,1,0:T(8,128)}) %reduce-scatter.15.cloned.1.call-update) | async-done | bytes 393232 | tf_op jit(solution)/shard_map/reduce_scatter | solution.py:46
  1287.4 17.8 %all_to_all.36 = f32[4,96,512]{2,1,0:T(8,128)} all-to-all(f32[4,96,512]{2,1,0:T(8,128)S(1)} %bitcast.168), channel_id=1, replica_groups=mesh['row_0'=2,'row_1'=2,'col_0'=4,'col_1'=2,'col_2'=4] {'row_0','row_1'}, dimensions={0} | all-to-all | bytes 1572864 | tf_op jit(solution)/shard_map/all_to_all | solution.py:62
  1311.1 11.8 gather_fusion.3
  1322.9 59.9 %all-gather.8.cloned.1.call-done = bf16[3072,512]{1,0:T(8,128)(2,1)} async-done(((bf16[96,512]{1,0:T(8,128)(2,1)}), bf16[3072,512]{1,0:T(8,128)(2,1)}) %all-gather.8.cloned.1.call-update) | async-done | bytes 3145744 | tf_op jit(solution)/shard_map/all_gather | solution.py:126
  1391.0 6.5 all-to-all-start.5
  1410.6 11.8 all-to-all-done.5
  1437.6 11.7 scatter_fusion.1
  1450.2 141.5 %all-reduce.12.cloned.1.call-done = f32[131072]{0:T(1024)} async-done(((f32[131072]{0:T(1024)}), f32[131072]{0:T(1024)}) %all-reduce.12.cloned.1.call-update) | async-done | bytes 524304
  1601.1 8.3 psum.157
  1615.4 8.6 psum.159
  (155 shorter events, 149.0 us)
Async XLA Ops:
  8.0 508.5 %copy-start = (bf16[8,256,256]{2,1,0:T(8,128)(2,1)S(1)}, bf16[8,256,256]{2,1,0:T(8,128)(2,1)}, u32[]{:S(2)}) copy-start(bf16[8,256,256]{2,1,0:T(8,128)(2,1)} %param.19) | copy-start | bytes 3145732
  8.0 339.4 %copy-start.10 = (bf16[128,384]{1,0:T(8,128)(2,1)S(1)}, bf16[128,384]{1,0:T(8,128)(2,1)}, u32[]{:S(2)}) copy-start(bf16[128,384]{1,0:T(8,128)(2,1)} %param.15) | copy-start | bytes 294916
  8.0 339.6 %copy-start.7 = (bf16[3072,128]{1,0:T(8,128)(2,1)S(1)}, bf16[3072,128]{1,0:T(8,128)(2,1)}, u32[]{:S(2)}) copy-start(bf16[3072,128]{1,0:T(8,128)(2,1)} %param.14) | copy-start | bytes 2359300
  9.8 337.6 %all-to-all-start = ((bf16[4,96,512]{2,1,0:T(8,128)(2,1)}), bf16[4,96,512]{2,1,0:T(8,128)(2,1)S(1)}, u32[]{:S(2)}, u32[]{:S(2)}) async-start(bf16[4,96,512]{2,1,0:T(8,128)(2,1)} %broadcast_in_dim.16), calls=%async_computation | async-start | bytes 786432 | tf_op jit(solution)/shard_map/all_to_all | solution.py:31
  14.7 409.1 %reduce-scatter.7.cloned.1.call-start = ((), (), s32[]{:S(2)}) async-start(), calls=%async_computation.14 | async-start | bytes 7864320 | tf_op jit(solution)/shard_map/reduce_scatter | solution.py:46
  364.6 112.8 %all-gather.4.cloned.1.call-start = ((), (), s32[]{:S(2)}) async-start(), calls=%async_computation.13 | async-start | bytes 3244032 | tf_op jit(solution)/shard_map/all_gather | solution.py:88
  365.1 114.7 %reduce-scatter.9.cloned.1.call-start = ((), (), s32[]{:S(2)}) async-start(), calls=%async_computation.15 | async-start | bytes 1966080 | tf_op jit(solution)/shard_map/reduce_scatter | solution.py:46
  423.8 77.8 %reduce-scatter.11.cloned.1.call-start = ((), (), s32[]{:S(2)}) async-start(), calls=%async_computation.16 | async-start | bytes 589824 | tf_op jit(solution)/shard_map/reduce_scatter | solution.py:46
  479.9 23.4 %copy-start.4 = (f32[512,512]{1,0:T(8,128)S(1)}, f32[512,512]{1,0:T(8,128)}, u32[]{:S(2)}) copy-start(f32[512,512]{1,0:T(8,128)} %param.17) | copy-start | bytes 3145732
  479.9 94.9 %all-gather.6.cloned.1.call-start = ((), (), s32[]{:S(2)}) async-start(), calls=%async_computation.17 | async-start | bytes 3244032 | tf_op jit(solution)/shard_map/all_gather | solution.py:126
  501.6 14.9 copy-start.11
  581.2 31.5 %all-to-all-start.2 = ((bf16[4,512,512]{2,1,0:T(8,128)(2,1)}), bf16[4,512,512]{2,1,0:T(8,128)(2,1)}, u32[]{:S(2)}, u32[]{:S(2)}) async-start(bf16[4,512,512]{2,1,0:T(8,128)(2,1)} %broadcast_in_dim.17), calls=%async_computation.5 | async-start | bytes 4194304 | tf_op jit(solution)/shard_map/all_to_all | solution.py:31
  587.7 5.6 copy-start.14
  587.7 6.3 copy-start.8
  587.7 6.3 copy-start.23
  594.0 18.6 %copy-start.16 = (bf16[96,512]{1,0:T(8,128)(2,1)S(1)}, bf16[96,512]{1,0:T(8,128)(2,1)}, u32[]{:S(2)}) copy-start(bf16[96,512]{1,0:T(8,128)(2,1)} %fusion.60) | copy-start | bytes 294916
  613.4 11.6 all-to-all-start.3
  618.3 164.1 %all-reduce.10.cloned.1.call-start = ((), (), s32[]{:S(2)}) async-start(), calls=%async_computation.22 | async-start | bytes 1048576
  627.9 154.6 %copy-start.20 = (f32[1024]{0:T(1024)S(1)}, f32[1024]{0:T(1024)}, u32[]{:S(2)}) copy-start(f32[1024]{0:T(1024)} %param.12) | copy-start | bytes 12292
  640.5 619.5 %reduce-scatter.13.cloned.1.call-start = ((), (), s32[]{:S(2)}) async-start(), calls=%async_computation.18 | async-start | bytes 7864320 | tf_op jit(solution)/shard_map/reduce_scatter | solution.py:46
  1202.7 84.3 %reduce-scatter.15.cloned.1.call-start = ((), (), s32[]{:S(2)}) async-start(), calls=%async_computation.19 | async-start | bytes 1966080 | tf_op jit(solution)/shard_map/reduce_scatter | solution.py:46
  1259.9 49.6 %reduce-scatter.17.cloned.1.call-start = ((), (), s32[]{:S(2)}) async-start(), calls=%async_computation.20 | async-start | bytes 589824 | tf_op jit(solution)/shard_map/reduce_scatter | solution.py:46
  1287.0 95.8 %all-gather.8.cloned.1.call-start = ((), (), s32[]{:S(2)}) async-start(), calls=%async_computation.21 | async-start | bytes 3244032 | tf_op jit(solution)/shard_map/all_gather | solution.py:126
  1391.0 31.4 %all-to-all-start.5 = ((bf16[4,512,512]{2,1,0:T(8,128)(2,1)}), bf16[4,512,512]{2,1,0:T(8,128)(2,1)}, u32[]{:S(2)}, u32[]{:S(2)}) async-start(bf16[4,512,512]{2,1,0:T(8,128)(2,1)} %broadcast_in_dim.21), calls=%async_computation.11 | async-start | bytes 4194304 | tf_op jit(solution)/shard_map/all_to_all | solution.py:31
  1403.0 6.2 copy-start.9
  1403.0 6.2 copy-start.24
  1409.3 13.2 copy-start.17
  1410.6 19.6 %copy-start.5 = (f32[512,512]{1,0:T(8,128)S(1)}, f32[512,512]{1,0:T(8,128)}, u32[]{:S(2)}) copy-start(f32[512,512]{1,0:T(8,128)} %param.17) | copy-start | bytes 3145732
  1410.6 19.6 %copy-start.6 = (f32[512,512]{0,1:T(8,128)S(1)}, f32[512,512]{0,1:T(8,128)}, u32[]{:S(2)}) copy-start(f32[512,512]{0,1:T(8,128)} %copy.61) | copy-start | bytes 3145732
  1423.3 11.6 all-to-all-start.6
  1428.2 163.4 %all-reduce.12.cloned.1.call-start = ((), (), s32[]{:S(2)}) async-start(), calls=%async_computation.23 | async-start | bytes 1048576
  1437.6 189.0 %copy-start.1 = (bf16[8,256,256]{2,1,0:T(8,128)(2,1)S(1)}, bf16[8,256,256]{2,1,0:T(8,128)(2,1)}, u32[]{:S(2)}) copy-start(bf16[8,256,256]{2,1,0:T(8,128)(2,1)} %param.19) | copy-start | bytes 3145732
  (9 other events, 26.9 us)
Sparse Core Ops, SparseCore 0:
  364.7 59.0 reduce-scatter.6
  426.2 26.8 reduce-scatter.8
  480.0 19.9 reduce-scatter.10
  1202.8 57.0 reduce-scatter.12
  1262.2 24.8 reduce-scatter.14
  1289.2 20.2 reduce-scatter.16
Sparse Core Ops, SparseCore 1:
  368.1 109.2 all-gather.3
  503.3 71.4 all-gather.5
  640.5 141.9 all-reduce.9
  1311.2 71.5 all-gather.7
  1450.3 141.3 all-reduce.11
where the time goes:
time: 1640 us; the launch traced here: 1630 us
  blocking collectives  795 us (48%)
  waiting for transfers between devices  623 us (38%)
  local copies, waits for them, and re-layouts  71.8 us (4%)
  matrix products  52.3 us (3%)
  other arithmetic  43.7 us (3%)
  starting transfers between devices  28.1 us (2%)
  between operations  20.3 us (1%)
    all_gather x2, blocking collectives, local(): all_duals = lax.all_gather(direction, ROW_COL, axis=0, tiled=True)  662 us
    unnamed x13, waiting for transfers between devices  284 us
    reduce_scatter x6, waiting for transfers between devices, sum_in_order(): parts = lax.psum_scatter(parts, axes[k], scatter_dimension=0, tiled=True)  146 us
    all_gather x2, waiting for transfers between devices, local(): field_rows = lax.all_gather(field_half, COL, axis=0, tiled=True)  107 us
    psum x15, blocking collectives, by_axis(): return functools.reduce(lax.psum, axes, array)  95 us
    all_gather x1, waiting for transfers between devices, local(): basis_rows = lax.all_gather(eigen_basis, COL, axis=0, tiled=True)  53.5 us
    all_to_all x2, blocking collectives, sent_and_summed(): lax.all_to_all(in_blocks(array, dim, length), axis, 0, 0, tiled=True)  37.9 us
  transfers between devices with their start and end apart: 16, of which 12 were waited for; matrix products, arithmetic and copies ran while one was open for 5% of the time, Pallas kernels for 0%

commit v1 on v0

v1 whole, which is shorter than its diff:
```python
import jax
import jax.numpy as jnp
from jax import lax
from jax.experimental import pallas as pl
from jax.experimental.pallas import tpu as pltpu
from jax.sharding import PartitionSpec as P

ITERS = 2
NR, NC = 4, 32
ND = NR * NC
MESH = pl.DeviceIdType.MESH
BF = jnp.bfloat16
F32 = jnp.float32
NN = (((1,), (0,)), ((), ()))
NT = (((1,), (1,)), ((), ()))
TN = (((0,), (0,)), ((), ()))


def dot(a, b, dims=NN):
    return lax.dot_general(a, b, dims, preferred_element_type=F32)


def pieces2(x):
    hi = x.astype(BF)
    return hi, (x - hi.astype(F32)).astype(BF)


def pieces3(x):
    hi = x.astype(BF)
    rest = x - hi.astype(F32)
    mid = rest.astype(BF)
    return hi, mid, (rest - mid.astype(F32)).astype(BF)


def place(q):
    rows = pl.ds(pl.multiple_of(lax.rem(q, 64) * 8, 8), 8)
    lanes = pl.ds(pl.multiple_of((q // 64) * 128, 128), 128)
    return rows, lanes


def spot(q):
    rows = pl.ds(pl.multiple_of((q // 4) * 16, 16), 16)
    lanes = pl.ds(pl.multiple_of(lax.rem(q, 4) * 128, 128), 128)
    return rows, lanes


def hots(owner):
    width = owner.shape[1]
    high = lax.shift_right_logical(owner, 7) & 511
    low = (lax.shift_right_logical(owner, 16) * 128) + (owner & 127)
    tall = jnp.where(lax.broadcasted_iota(jnp.int32, (512, width), 0) == high, 1.0, 0.0)
    wide = jnp.where(lax.broadcasted_iota(jnp.int32, (256, width), 0) == low, 1.0, 0.0)
    return tall.astype(BF), wide.astype(BF)


def fetch(d3, tall, wide):
    g = dot(d3, wide)
    g = g[:512] + g[512:1024] + g[1024:]
    return jnp.sum(g * tall.astype(F32), axis=0, keepdims=True)


def spread(values, tall, wide):
    x3 = jnp.concatenate(pieces3(wide.astype(F32) * values), axis=0)
    t = dot(tall, x3, NT)
    return t[:, :256] + t[:, 256:512] + t[:, 512:]


def kernel(
    rhs, p_own, u_in, v_in, own_t, own_l, omega, damp, damp_c, l_basis, l_omega, l_left, l_right,
    sol_out, res_out,
    p_rows, p_cols, u_own, v_own, vp_all, up_all, at, bt, sym, tall_l, wide_l, tall_t, wide_t,
    quad, full, vec, ret, d3, c_l, c_col, c_row, part_out, part_in, part4_out, part4_in,
    s_buf, k_out, k_in, k_red, k_full, tot, t_in, t_red, dir_own, rr_buf, ssem, rsem, lsem,
):
    i = lax.axis_index("row")
    j = lax.axis_index("col")
    me = i * NC + j
    x = j // 8
    h = lax.rem(j // 4, 2)
    z = lax.rem(j, 4)

    def line(r):
        return (i, lax.rem(j + r, NC))

    def file(r):
        return (lax.rem(i + r, NR), j)

    def dev(xx, hh, zz):
        return (i, xx * 8 + hh * 4 + zz)

    def send(src, dst, k, where):
        pltpu.make_async_remote_copy(
            src, dst, ssem.at[k], rsem.at[k], device_id=where, device_id_type=MESH
        ).start()

    def got(ref, k):
        pltpu.make_async_copy(ref, ref, rsem.at[k]).wait()

    def gone(ref, k):
        pltpu.make_async_copy(ref, ref, ssem.at[k]).wait()

    def everyone(body):
        def step(r, carry):
            o = lax.rem(me + r, ND)
            body(o, (o // NC, lax.rem(o, NC)))
            return carry

        lax.fori_loop(1, ND, step, 0)

    barrier = pltpu.get_barrier_semaphore()
    everyone(
        lambda o, where: pl.semaphore_signal(
            barrier, inc=1, device_id=where, device_id_type=MESH
        )
    )
    pl.semaphore_wait(barrier, ND - 1)

    lane_i = pl.ds(pl.multiple_of(i * 128, 128), 128)
    lane_j = pl.ds(pl.multiple_of(j * 128, 128), 128)
    for r in range(1, NR):
        o = lax.rem(i + r, NR)
        send(p_own, p_cols.at[i], 0, (o, j))
        send(v_in.at[o], v_own.at[:, lane_i], 1, (o, j))
    my_rows, my_lanes = place(me)
    everyone(lambda o, where: send(rhs, vec.at[my_rows, my_lanes], 3, where))
    half = 48
    A, B = pl.ds(0, half), pl.ds(half, half)
    send(p_own, p_rows.at[x, h, z], 4, dev(x, 1 - h, z))
    for r in (1, 3, 2):
        send(p_own.at[A], p_rows.at[x, h, z, A], 5, dev(x, h, lax.rem(z + r, 4)))
        send(p_own.at[B], p_rows.at[x, h, z, B], 5, dev(lax.rem(x + r, 4), h, z))

    p_cols[i] = p_own[...]
    p_rows[x, h, z] = p_own[...]
    v_own[:, lane_i] = v_in[i]
    vec[my_rows, my_lanes] = rhs[...]

    got(p_rows.at[0, 0, 0], 4)
    for r in (1, 3, 2):
        send(p_rows.at[x, 1 - h, z, A], p_rows.at[x, 1 - h, z, A], 5, dev(x, h, lax.rem(z + r, 4)))
        send(p_rows.at[x, 1 - h, z, B], p_rows.at[x, 1 - h, z, B], 5, dev(lax.rem(x + r, 4), h, z))

    got(p_cols.at[pl.ds(0, 3)], 0)
    vp = dot(v_in[...].reshape(384, 128), p_cols[...].reshape(384, 512), TN).astype(BF)
    vp_all[x, h, z] = vp

    tall, wide = hots(own_t[...])
    tall_t[...] = tall
    wide_t[...] = wide

    got(p_rows.at[pl.ds(0, 3), :, 0], 5)
    for r in (1, 3, 2):
        send(p_rows.at[x, :, :, A], p_rows.at[x, :, :, A], 6, dev(lax.rem(x + r, 4), h, z))
        send(p_rows.at[:, :, z, B], p_rows.at[:, :, z, B], 6, dev(x, h, lax.rem(z + r, 4)))

    def u_send(r, carry):
        o = lax.rem(j + r, NC)
        send(u_in.at[o], u_own.at[:, lane_j], 2, (i, o))
        return carry

    C, D = pl.ds(0, 64), pl.ds(64, 64)
    send(vp_all.at[x, h, z], vp_all.at[x, h, z], 7, dev(x, 1 - h, z))
    for r in (1, 3, 2):
        send(vp_all.at[x, h, z, C], vp_all.at[x, h, z, C], 8, dev(x, h, lax.rem(z + r, 4)))
        send(vp_all.at[x, h, z, D], vp_all.at[x, h, z, D], 8, dev(lax.rem(x + r, 4), h, z))
    lax.fori_loop(1, NC, u_send, 0)
    u_own[:, lane_j] = u_in[j]

    def prepare(b, carry):
        basis = l_basis[b]
        at[b] = dot(l_left[b], basis).T.astype(BF)
        bt[b] = dot(l_right[b], basis).T.astype(BF)
        om = l_omega[b]
        sym[b] = 0.5 * (om + om.T)
        tall, wide = hots(own_l[pl.ds(b, 1), :])
        tall_l[b] = tall
        wide_l[b] = wide
        return carry

    got(vp_all.at[0, 0, 0], 7)
    for r in (1, 3, 2):
        send(vp_all.at[x, 1 - h, z, C], vp_all.at[x, 1 - h, z, C], 8, dev(x, h, lax.rem(z + r, 4)))
        send(vp_all.at[x, 1 - h, z, D], vp_all.at[x, 1 - h, z, D], 8, dev(lax.rem(x + r, 4), h, z))
    lax.fori_loop(0, 4, prepare, 0)
    got(vp_all.at[pl.ds(0, 3), :, 0], 8)
    for r in (1, 3, 2):
        send(vp_all.at[x, :, :, C], vp_all.at[x, :, :, C], 9, dev(lax.rem(x + r, 4), h, z))
        send(vp_all.at[:, :, z, D], vp_all.at[:, :, z, D], 9, dev(x, h, lax.rem(z + r, 4)))

    got(p_rows.at[pl.ds(0, 3)], 6)

    def project(k, acc):
        u = u_in[pl.ds(k * 8, 8)].reshape(768, 128)
        return acc + dot(u, p_rows[k].reshape(768, 512), TN)

    up = lax.fori_loop(0, 4, project, jnp.zeros((128, 512), F32)).astype(BF)
    up_all[i] = up
    for r in range(1, NR):
        send(up_all.at[i], up_all.at[i], 10, file(r))

    lax.fori_loop(4, 8, prepare, 0)
    om = omega[...]
    quad[...] = 0.5 * (om + om.T) - damp[...] - damp_c[...]

    got(t_in.at[pl.ds(0, ND - 1)], 3)
    first = vec[...]
    ret[...] = first
    dir_own[...] = rhs[...]
    res_out[...] = rhs[...]
    sol_out[...] = jnp.zeros_like(rhs)
    rr_buf[...] = jnp.broadcast_to(jnp.sum(first * first, keepdims=True), (8, 128))

    def iterate(it, carry):
        d3[...] = jnp.concatenate(pieces3(vec[...]), axis=0)
        c_own = jnp.broadcast_to(fetch(d3[...], tall_t[...], wide_t[...]), (8, 128))
        c_col[j] = c_own
        c_row[i] = c_own

        def c_send(r, carry):
            send(c_col.at[j], c_col.at[j], 11, line(r))
            return carry

        lax.fori_loop(1, NC, c_send, 0)
        for r in range(1, NR):
            send(c_row.at[i], c_row.at[i], 12, file(r))

        def take(b, carry):
            c_l[b] = jnp.broadcast_to(fetch(d3[...], tall_l[b], wide_l[b]), (8, 256))
            return carry

        lax.fori_loop(0, 8, take, 0)

        @pl.when(it == 0)
        def _():
            got(vp_all.at[pl.ds(0, 3)], 9)
            got(u_own.at[:, pl.ds(0, 31 * 128)], 2)
            got(up_all.at[pl.ds(0, 3)], 10)
            got(v_own.at[:, pl.ds(0, 384)], 1)

        got(c_col.at[pl.ds(0, NC - 1)], 11)
        got(c_row.at[pl.ds(0, NR - 1)], 12)
        gone(c_col.at[pl.ds(0, NC - 1)], 11)
        gone(c_row.at[pl.ds(0, NR - 1)], 12)

        def add_rows(k, acc):
            lanes = pl.ds(pl.multiple_of(k * 1024, 1024), 1024)
            c = c_col[pl.ds(k * 8, 8)]
            c = jnp.concatenate([c[n, :1] for n in range(8)], axis=0).T
            v = vp_all[k].reshape(8, 128, 512)
            sv = [(v[n].astype(F32) * c[:, n : n + 1]).astype(BF) for n in range(8)]
            return acc + dot(u_own[:, lanes], jnp.concatenate(sv, axis=0))

        c = c_row[...]
        c = jnp.concatenate([c[n, :1] for n in range(NR)] * 2, axis=0).T
        su = [(up_all[n].astype(F32) * c[:, n : n + 1]).astype(BF) for n in range(NR)]
        s = lax.fori_loop(0, 4, add_rows, dot(v_own[...], jnp.concatenate(su, axis=0)))
        s = s.astype(BF)
        k_out[...] = dot(p_own[...], s, TN).astype(BF)

        def k_send(o, where):
            rows, lanes = spot(o)
            send(k_out.at[rows, lanes], k_in.at[me], 13, where)

        everyone(k_send)
        k_rows, k_lanes = spot(me)
        k_in[me] = k_out[k_rows, k_lanes]

        s_buf[...] = jnp.concatenate(pieces2(s.astype(F32) * damp[...]), axis=0)

        def field(k, carry):
            lanes = pl.ds(pl.multiple_of(k * 1024, 1024), 1024)
            t = dot(s_buf[...], vp_all[k].reshape(1024, 512), NT)
            t = (t[:96] + t[96:]) * u_own[:, lanes].astype(F32)
            t = jnp.sum(t, axis=0, keepdims=True)
            for n in range(8):
                part_out[k * 8 + n] = jnp.broadcast_to(t[:, n * 128 : (n + 1) * 128], (8, 128))
            return carry

        lax.fori_loop(0, 4, field, 0)
        t = dot(s_buf[...], up_all[...].reshape(512, 512), NT)
        t = jnp.sum((t[:96] + t[96:]) * v_own[...].astype(F32), axis=0, keepdims=True)
        for n in range(NR):
            part4_out[n] = jnp.broadcast_to(t[:, n * 128 : (n + 1) * 128], (8, 128))

        def part_send(r, carry):
            o = lax.rem(j + r, NC)
            send(part_out.at[o], part_in.at[j], 14, (i, o))
            return carry

        lax.fori_loop(1, NC, part_send, 0)
        for r in range(1, NR):
            o = lax.rem(i + r, NR)
            send(part4_out.at[o], part4_in.at[i], 15, (o, j))
        part_in[j] = part_out[j]
        part4_in[i] = part4_out[i]

        tot[...] = jnp.zeros((512, 256), F32)

        def blocks(b, carry):
            a = at[b].astype(F32)
            right = bt[b]
            hi, lo = pieces2(a * c_l[b][:1])
            half_t = dot(hi, right, NT) + dot(lo, right, NT)
            w = sym[b] * (half_t + half_t.T)
            hi, lo = pieces2(w)
            mixed = dot(hi, right) + dot(lo, right)
            values = 2.0 * jnp.sum(a * mixed, axis=0, keepdims=True)
            tot[...] += spread(values, tall_l[b], wide_l[b])
            return carry

        lax.fori_loop(0, 4, blocks, 0)

        got(k_in.at[pl.ds(0, ND - 1)], 13)
        k_red[...] = jnp.sum(k_in[...].astype(F32), axis=0).astype(BF)
        everyone(lambda o, where: send(k_red, k_full.at[k_rows, k_lanes], 16, where))
        k_full[k_rows, k_lanes] = k_red[...]
        lax.fori_loop(4, 8, blocks, 0)

        got(k_in.at[pl.ds(0, ND - 1)], 16)
        gone(k_in.at[pl.ds(0, ND - 1)], 13)
        gone(k_in.at[pl.ds(0, ND - 1)], 16)
        hi, lo = pieces2(k_full[...].astype(F32) * quad[...])
        y = dot(vp_all[x, h, z], hi) + dot(vp_all[x, h, z], lo)
        y = y * up_all[i].astype(F32)
        y = y[:, :128] + y[:, 128:256] + y[:, 256:384] + y[:, 384:]
        y = jnp.sum(y.T, axis=0, keepdims=True)
        got(part_in.at[pl.ds(0, NC - 1)], 14)
        got(part4_in.at[pl.ds(0, NR - 1)], 15)
        gone(part_in.at[pl.ds(0, NC - 1)], 14)
        gone(part4_in.at[pl.ds(0, NR - 1)], 15)
        parts = jnp.sum(part_in[...], axis=0) + jnp.sum(part4_in[...], axis=0)
        tot[...] += spread(2.0 * (y + parts[:1]), tall_t[...], wide_t[...])

        def t_send(o, where):
            rows, lanes = place(o)
            send(tot.at[rows, lanes], t_in.at[me], 17, where)

        everyone(t_send)
        t_in[me] = tot[my_rows, my_lanes]
        got(t_in.at[pl.ds(0, ND - 1)], 17)
        t_red[...] = jnp.sum(t_in[...], axis=0)
        gone(t_in.at[pl.ds(0, ND - 1)], 17)
        everyone(lambda o, where: send(t_red, full.at[my_rows, my_lanes], 18, where))
        full[my_rows, my_lanes] = t_red[...]
        got(t_in.at[pl.ds(0, ND - 1)], 18)
        gone(t_in.at[pl.ds(0, ND - 1)], 18)

        direction = vec[...]
        applied = direction + full[...]
        rr = rr_buf[...]
        step = rr / jnp.broadcast_to(jnp.sum(direction * applied, keepdims=True), (8, 128))
        sol_out[...] += step * dir_own[...]
        res_out[...] -= step * (dir_own[...] + t_red[...])
        res = ret[...] - step[:1, :1] * applied
        ret[...] = res
        new = jnp.broadcast_to(jnp.sum(res * res, keepdims=True), (8, 128))
        beta = new / rr
        vec[...] = res + beta[:1, :1] * direction
        dir_own[...] = res_out[...] + beta * dir_own[...]
        rr_buf[...] = new
        return carry

    lax.fori_loop(0, ITERS, iterate, 0)

    gone(p_cols.at[pl.ds(0, 3)], 0)
    gone(v_own.at[:, pl.ds(0, 384)], 1)
    gone(u_own.at[:, pl.ds(0, 31 * 128)], 2)
    gone(t_in.at[pl.ds(0, ND - 1)], 3)
    gone(p_rows.at[0, 0, 0], 4)
    gone(p_rows.at[pl.ds(0, 3), :, 0], 5)
    gone(p_rows.at[pl.ds(0, 3)], 6)
    gone(vp_all.at[0, 0, 0], 7)
    gone(vp_all.at[pl.ds(0, 3), :, 0], 8)
    gone(vp_all.at[pl.ds(0, 3)], 9)
    gone(up_all.at[pl.ds(0, 3)], 10)


def local(
    right_side, eigen_basis, tile_left, tile_right, piece_owner, omega_main, damping,
    local_basis, local_omega, local_left, local_right, local_owner,
):
    vmem = pl.BlockSpec(memory_space=pltpu.VMEM)
    V = pltpu.VMEM
    chunk = jax.ShapeDtypeStruct((8, 128), F32)
    scratch = [
        V((4, 2, 4, 96, 512), BF),
        V((4, 96, 512), BF),
        V((96, 4096), BF),
        V((96, 512), BF),
        V((4, 2, 4, 128, 512), BF),
        V((4, 128, 512), BF),
        V((8, 256, 256), BF),
        V((8, 256, 256), BF),
        V((8, 256, 256), F32),
        V((8, 512, 256), BF),
        V((8, 256, 256), BF),
        V((512, 128), BF),
        V((256, 128), BF),
        V((512, 512), F32),
        V((512, 256), F32),
        V((512, 256), F32),
        V((512, 256), F32),
        V((1536, 256), BF),
        V((8, 8, 256), F32),
        V((32, 8, 128), F32),
        V((4, 8, 128), F32),
        V((32, 8, 128), F32),
        V((32, 8, 128), F32),
        V((4, 8, 128), F32),
        V((4, 8, 128), F32),
        V((192, 512), BF),
        V((512, 512), BF),
        V((128, 16, 128), BF),
        V((16, 128), BF),
        V((512, 512), BF),
        V((512, 256), F32),
        V((128, 8, 128), F32),
        V((8, 128), F32),
        V((8, 128), F32),
        V((8, 128), F32),
        pltpu.SemaphoreType.DMA((19,)),
        pltpu.SemaphoreType.DMA((19,)),
        pltpu.SemaphoreType.DMA((2,)),
    ]
    out = pl.pallas_call(
        kernel,
        out_shape=(chunk, chunk),
        in_specs=[vmem] * 13,
        out_specs=(vmem, vmem),
        scratch_shapes=scratch,
        name="newton",
        compiler_params=pltpu.CompilerParams(
            collective_id=0, has_side_effects=True, vmem_limit_bytes=56 * 1024 * 1024
        ),
    )(
        right_side.reshape(8, 128),
        eigen_basis,
        tile_left.reshape(32, 96, 128),
        tile_right.T.reshape(4, 96, 128),
        piece_owner,
        local_owner,
        omega_main,
        damping.reshape(1, 512),
        damping.reshape(512, 1),
        local_basis,
        local_omega,
        local_left,
        local_right,
    )
    return out[0].reshape(-1), out[1].reshape(-1)


def solution(mesh):
    both = ("row", "col")
    placed = (
        P(both), P(both, None), P("row", "col"), P("row", "col"), P("row", "col"), P(), P(),
        P(both, None, None), P(both, None, None), P(both, None, None), P(both, None, None),
        P(both, None),
    )
    return jax.shard_map(
        local, mesh=mesh, in_specs=placed, out_specs=(P(both), P(both)), check_vma=False
    )
```

time: 1640 us -> 200 us (0.12)
  blocking collectives: 795 us -> 0 us
  waiting for transfers between devices: 623 us -> 0 us
  Pallas kernels: 0 us -> 193 us
  local copies, waits for them, and re-layouts: 71.8 us -> 5.7 us
  matrix products: 52.3 us -> 0 us
  other arithmetic: 43.7 us -> 0 us
  starting transfers between devices: 28.1 us -> 0 us
  between operations: 20.3 us -> 0.64 us
    all_gather x2 -> x0, blocking collectives: 662 us -> none  [local(): all_duals = lax.all_gather(direction, ROW_COL, axis=0, tiled=True)]
    unnamed x13 -> x0, waiting for transfers between devices: 284 us -> none
    pallas_call x0 -> x1, Pallas kernels: none -> 193 us  [local(): pl.pallas_call(kernel, out_shape=(chunk, chunk), in_specs=[vmem] * 13, ou...]
    all_gather x3 -> x0, waiting for transfers between devices: 161 us -> none  [the longest x2 107 us: local(): field_rows = lax.all_gather(field_half, COL, axis=0, tiled=True)]
    reduce_scatter x6 -> x0, waiting for transfers between devices: 146 us -> none  [sum_in_order(): parts = lax.psum_scatter(parts, axes[k], scatter_dimension=0, tiled=True)]
    psum x15 -> x0, blocking collectives: 95 us -> none  [by_axis(): return functools.reduce(lax.psum, axes, array)]
    dot_general x24 -> x0, matrix products: 52.3 us -> none  [the longest x2 11.1 us: local(): jnp.einsum('lpb,lba->lpa', right_float, local_w, precision=precise)]
    all_to_all x2 -> x0, blocking collectives: 37.9 us -> none  [sent_and_summed(): lax.all_to_all(in_blocks(array, dim, length), axis, 0, 0, tiled=True)]
  transfers between devices with their start and end apart: 16 -> 0, of which waited for: 12 -> 0; matrix products, arithmetic and copies ran while one was open for 5% -> 0% of each run, Pallas kernels for 0% -> 0%
where the time goes in v1:
time: 200 us; the launch traced here: 199 us
  Pallas kernels  193 us (96%)
  local copies, waits for them, and re-layouts  5.7 us (3%)
    pallas_call x1, Pallas kernels, local(): pl.pallas_call(kernel, out_shape=(chunk, chunk), in_specs=[vmem] * 13, ou...  193 us

profile of v1, /device:TPU:1, one launch (start us, length us, event | category | flops | bytes accessed | tf_op | source)
XLA Modules:
  0.0 199.3 jit_solution(15002198387658425037)
XLA Ops:
  0.6 1.6 copy.15
  2.3 1.5 copy.16.damp_c
  3.8 193.0 %newton.1 = (f32[8,128]{1,0:T(8,128)}, f32[8,128]{1,0:T(8,128)}) custom-call(f32[8,128]{1,0:T(8,128)} %bitcast.13, bf16[96,512]{1,0:T(8,128)(2,1)} %p_own.1, bf16[32,96,128]{2,1,0:T(8,128)(2,1)} %bitcast.8, bf16[4,96,128]{2,1,0:T(8,128)(2,1)} %bitcast.9, s32[1,128]{1,0:T(1,128)} %own_t.1, s32[8,256]{1,0:T(8,128)} %own_l.1, f32[512,512]{1,0:T(8,128)} %omega.1, ...), custom_call_target="tpu_custom_call" | custom-call | tf_op jit(solution)/shard_map/newton/pallas_call | solution.py:425
  196.8 1.3 copy.19
  198.0 1.3 copy.20

commit v2 on v1

v2 whole, which is shorter than its diff:
```python
import jax
import jax.numpy as jnp
from jax import lax
from jax.experimental import pallas as pl
from jax.experimental.pallas import tpu as pltpu
from jax.sharding import PartitionSpec as P

ITERS = 2
NR, NC = 4, 32
ND = NR * NC
MESH = pl.DeviceIdType.MESH
BF = jnp.bfloat16
F32 = jnp.float32
NN = (((1,), (0,)), ((), ()))
NT = (((1,), (1,)), ((), ()))
TN = (((0,), (0,)), ((), ()))


def dot(a, b, dims=NN):
    return lax.dot_general(a, b, dims, preferred_element_type=F32)


def pieces2(x):
    hi = x.astype(BF)
    return hi, (x - hi.astype(F32)).astype(BF)


def pieces3(x):
    hi = x.astype(BF)
    rest = x - hi.astype(F32)
    mid = rest.astype(BF)
    return hi, mid, (rest - mid.astype(F32)).astype(BF)


def place(q):
    rows = pl.ds(pl.multiple_of(lax.rem(q, 64) * 8, 8), 8)
    lanes = pl.ds(pl.multiple_of((q // 64) * 128, 128), 128)
    return rows, lanes


def spot(q):
    rows = pl.ds(pl.multiple_of((q // 4) * 16, 16), 16)
    lanes = pl.ds(pl.multiple_of(lax.rem(q, 4) * 128, 128), 128)
    return rows, lanes


def hots(owner):
    width = owner.shape[1]
    high = lax.shift_right_logical(owner, 7) & 511
    low = (lax.shift_right_logical(owner, 16) * 128) + (owner & 127)
    tall = jnp.where(lax.broadcasted_iota(jnp.int32, (512, width), 0) == high, 1.0, 0.0)
    wide = jnp.where(lax.broadcasted_iota(jnp.int32, (256, width), 0) == low, 1.0, 0.0)
    return tall.astype(BF), wide.astype(BF)


def fetch(d3, tall, wide):
    g = dot(d3, wide)
    g = g[:512] + g[512:1024] + g[1024:]
    return jnp.sum(g * tall.astype(F32), axis=0, keepdims=True)


def spread(values, tall, wide):
    x3 = jnp.concatenate(pieces3(wide.astype(F32) * values), axis=0)
    t = dot(tall, x3, NT)
    return t[:, :256] + t[:, 256:512] + t[:, 512:]


def kernel(
    rhs, p_own, u_in, v_raw, own_in, own_l, omega, damp, hbm_basis, hbm_omega, hbm_left, hbm_right,
    out,
    l_basis, l_omega, l_left, l_right, v_in, v_tile, u_tile, own_t,
    p_rows, p_cols, u_own, v_own, vp_all, up_all, at, bt, sym, tall_l, wide_l, tall_t, wide_t,
    quad, full, vec, ret, d3, c_l, c_col, c_row, part_out, part_in, part4_out, part4_in,
    s_buf, k_out, k_in, k_red, k_full, tot, t_in, t_red, s_out, s_in, dir_own, rr_buf,
    ssem, rsem, lsem,
):
    row = lax.axis_index("row")
    col = lax.axis_index("col")
    me = row * NC + col
    x = col // 8
    h = lax.rem(col // 4, 2)
    z = lax.rem(col, 4)
    core = lax.rem(row, 2)
    i = (row // 2) * 2 + h
    j = x * 8 + core * 4 + z
    moved = core != h
    kept = core == h

    def holder(ii, jj):
        return (
            (ii // 2) * 2 + lax.rem(jj // 4, 2),
            (jj // 8) * 8 + lax.rem(ii, 2) * 4 + lax.rem(jj, 4),
        )

    def line(r):
        return holder(i, lax.rem(j + r, NC))

    def file(r):
        return holder(lax.rem(i + r, NR), j)

    def dev(xx, zz):
        return (row, xx * 8 + h * 4 + zz)

    sibling = (row + 1 - 2 * core, col)

    def send(src, dst, k, where):
        pltpu.make_async_remote_copy(
            src, dst, ssem.at[k], rsem.at[k], device_id=where, device_id_type=MESH
        ).start()

    def got(ref, k):
        pltpu.make_async_copy(ref, ref, rsem.at[k]).wait()

    def gone(ref, k):
        pltpu.make_async_copy(ref, ref, ssem.at[k]).wait()

    def everyone(body):
        def step(r, carry):
            o = lax.rem(me + r, ND)
            body(o, (o // NC, lax.rem(o, NC)))
            return carry

        lax.fori_loop(1, ND, step, 0)

    loads = [
        pltpu.make_async_copy(src, dst, lsem.at[n])
        for n, (src, dst) in enumerate(
            [(hbm_basis, l_basis), (hbm_left, l_left), (hbm_right, l_right), (hbm_omega, l_omega)]
        )
    ]
    for load in loads:
        load.start()
    v_in[...] = v_raw[...].astype(F32).T.astype(BF).reshape(4, 96, 128)

    barrier = pltpu.get_barrier_semaphore()
    everyone(
        lambda o, where: pl.semaphore_signal(
            barrier, inc=1, device_id=where, device_id_type=MESH
        )
    )
    pl.semaphore_wait(barrier, ND - 1)

    lane_row = pl.ds(pl.multiple_of(row * 128, 128), 128)
    lane_col = pl.ds(pl.multiple_of(col * 128, 128), 128)
    for r in range(1, NR):
        o = lax.rem(row + r, NR)
        send(p_own, p_cols.at[row], 0, holder(o, col))

    @pl.when(moved)
    def _():
        send(p_own, p_cols.at[row], 19, holder(row, col))
        send(v_in, v_tile, 21, holder(row, col))
        send(own_in, own_t, 22, holder(row, col))

    @pl.when(kept)
    def _():
        p_cols[row] = p_own[...]
        v_tile[...] = v_in[...]
        own_t[...] = own_in[...]

    got(p_cols.at[pl.ds(0, 3)], 0)

    @pl.when(moved)
    def _():
        got(p_cols.at[0], 19)
        got(v_tile, 21)
        got(own_t, 22)

    A, B = pl.ds(0, 48), pl.ds(48, 48)
    for r in (1, 3, 2):
        send(p_cols.at[i, A], p_rows.at[x, core, z, A], 5, dev(x, lax.rem(z + r, 4)))
        send(p_cols.at[i, B], p_rows.at[x, core, z, B], 5, dev(lax.rem(x + r, 4), z))
    p_rows[x, core, z] = p_cols[i]

    vp = dot(v_tile[...].reshape(384, 128), p_cols[...].reshape(384, 512), TN).astype(BF)
    vp_all[x, core, z] = vp

    my_rows, my_lanes = place(me)
    everyone(lambda o, where: send(rhs, vec.at[my_rows, my_lanes], 3, where))
    vec[my_rows, my_lanes] = rhs[...]

    got(p_rows.at[pl.ds(0, 3), 0, 0], 5)
    for r in (1, 3, 2):
        send(p_rows.at[x, core, :, A], p_rows.at[x, core, :, A], 6, dev(lax.rem(x + r, 4), z))
        send(p_rows.at[:, core, z, B], p_rows.at[:, core, z, B], 6, dev(x, lax.rem(z + r, 4)))

    @pl.when(moved)
    def _():
        send(u_in, u_tile, 23, holder(row, col))

    @pl.when(kept)
    def _():
        pltpu.make_async_copy(u_in, u_tile, lsem.at[4]).start()

    C, D = pl.ds(0, 64), pl.ds(64, 64)
    for r in (1, 3, 2):
        send(vp_all.at[x, core, z, C], vp_all.at[x, core, z, C], 8, dev(x, lax.rem(z + r, 4)))
        send(vp_all.at[x, core, z, D], vp_all.at[x, core, z, D], 8, dev(lax.rem(x + r, 4), z))
    for r in range(1, NR):
        o = lax.rem(row + r, NR)
        send(v_in.at[o], v_own.at[:, lane_row], 1, holder(o, col))

    def u_send(r, carry):
        o = lax.rem(col + r, NC)
        send(u_in.at[o], u_own.at[:, lane_col], 2, holder(row, o))
        return carry

    lax.fori_loop(1, NC, u_send, 0)

    @pl.when(moved)
    def _():
        send(v_in.at[row], v_own.at[:, lane_row], 20, holder(row, col))
        send(u_in.at[col], u_own.at[:, lane_col], 24, holder(row, col))

    @pl.when(kept)
    def _():
        v_own[:, lane_row] = v_in[row]
        pltpu.make_async_copy(u_in.at[col], u_own.at[:, lane_col], lsem.at[5]).start()

    def prepare(b, carry):
        basis = l_basis[b]
        at[b] = dot(l_left[b], basis).T.astype(BF)
        bt[b] = dot(l_right[b], basis).T.astype(BF)
        om = l_omega[b]
        sym[b] = 0.5 * (om + om.T)
        tall, wide = hots(own_l[pl.ds(b, 1), :])
        tall_l[b] = tall
        wide_l[b] = wide
        return carry

    tall, wide = hots(own_t[...])
    tall_t[...] = tall
    wide_t[...] = wide
    for load in loads:
        load.wait()

    def spread_c():
        d3[...] = jnp.concatenate(pieces3(vec[...]), axis=0)
        c_own = jnp.broadcast_to(fetch(d3[...], tall_t[...], wide_t[...]), (8, 128))
        c_col[j] = c_own
        c_row[i] = c_own

        def c_send(r, carry):
            send(c_col.at[j, pl.ds(0, 1)], c_col.at[j, pl.ds(0, 1)], 11, line(r))
            return carry

        lax.fori_loop(1, NC, c_send, 0)
        for r in range(1, NR):
            send(c_row.at[i, pl.ds(0, 1)], c_row.at[i, pl.ds(0, 1)], 12, file(r))

    def take(b, carry):
        c_l[b] = jnp.broadcast_to(fetch(d3[...], tall_l[b], wide_l[b]), (8, 256))
        return carry

    lax.fori_loop(0, 2, prepare, 0)
    got(vp_all.at[pl.ds(0, 3), 0, 0], 8)
    for r in (1, 3, 2):
        send(vp_all.at[x, core, :, C], vp_all.at[x, core, :, C], 9, dev(lax.rem(x + r, 4), z))
        send(vp_all.at[:, core, z, D], vp_all.at[:, core, z, D], 9, dev(x, lax.rem(z + r, 4)))
    got(p_rows.at[:, 0, pl.ds(0, 3)], 6)
    send(p_rows.at[:, core], p_rows.at[:, core], 4, sibling)

    got(t_in.at[pl.ds(0, ND - 1)], 3)
    first = vec[...]
    ret[...] = first
    dir_own[...] = rhs[...]
    out[1] = rhs[...]
    out[0] = jnp.zeros_like(rhs)
    rr_buf[...] = jnp.broadcast_to(jnp.sum(first * first, keepdims=True), (8, 128))
    spread_c()
    lax.fori_loop(2, 5, prepare, 0)

    got(p_rows.at[:, 0], 4)

    @pl.when(moved)
    def _():
        got(u_tile, 23)

    @pl.when(kept)
    def _():
        pltpu.make_async_copy(u_in, u_tile, lsem.at[4]).wait()

    def project(k, acc):
        u = u_tile[pl.ds(k * 8, 8)].reshape(768, 128)
        return acc + dot(u, p_rows[k].reshape(768, 512), TN)

    up = lax.fori_loop(0, 4, project, jnp.zeros((128, 512), F32)).astype(BF)
    up_all[i] = up
    for r in range(1, NR):
        send(up_all.at[i], up_all.at[i], 10, file(r))

    got(vp_all.at[:, 0, pl.ds(0, 3)], 9)
    send(vp_all.at[:, core], vp_all.at[:, core], 7, sibling)
    lax.fori_loop(5, 8, prepare, 0)
    t = 0.5 * omega[...] - damp[...]
    quad[...] = t + t.T
    lax.fori_loop(0, 8, take, 0)

    got(u_own.at[:, pl.ds(0, 31 * 128)], 2)
    got(v_own.at[:, pl.ds(0, 384)], 1)

    @pl.when(moved)
    def _():
        got(v_own.at[:, pl.ds(0, 128)], 20)
        got(u_own.at[:, pl.ds(0, 128)], 24)

    @pl.when(kept)
    def _():
        pltpu.make_async_copy(u_in.at[col], u_own.at[:, lane_col], lsem.at[5]).wait()

    got(vp_all.at[:, 0], 7)
    got(up_all.at[pl.ds(0, 3)], 10)

    def iterate(it, carry):
        got(c_col.at[pl.ds(0, NC - 1), pl.ds(0, 1)], 11)
        got(c_row.at[pl.ds(0, NR - 1), pl.ds(0, 1)], 12)
        gone(c_col.at[pl.ds(0, NC - 1), pl.ds(0, 1)], 11)
        gone(c_row.at[pl.ds(0, NR - 1), pl.ds(0, 1)], 12)

        def add_rows(k, acc):
            lanes = pl.ds(pl.multiple_of(k * 1024, 1024), 1024)
            c = c_col[pl.ds(k * 8, 8)]
            c = jnp.concatenate([c[n, :1] for n in range(8)], axis=0).T
            v = vp_all[k].reshape(8, 128, 512)
            sv = [(v[n].astype(F32) * c[:, n : n + 1]).astype(BF) for n in range(8)]
            return acc + dot(u_own[:, lanes], jnp.concatenate(sv, axis=0))

        c = c_row[...]
        c = jnp.concatenate([c[n, :1] for n in range(NR)] * 2, axis=0).T
        su = [(up_all[n].astype(F32) * c[:, n : n + 1]).astype(BF) for n in range(NR)]
        s = lax.fori_loop(0, 4, add_rows, dot(v_own[...], jnp.concatenate(su, axis=0)))
        s = s.astype(BF)
        k_out[...] = dot(p_cols[i], s, TN).astype(BF)

        def k_send(o, where):
            rows, lanes = spot(o)
            send(k_out.at[rows, lanes], k_in.at[me], 13, where)

        everyone(k_send)
        k_rows, k_lanes = spot(me)
        k_in[me] = k_out[k_rows, k_lanes]

        s_buf[...] = jnp.concatenate(pieces2(s.astype(F32) * damp[...]), axis=0)

        def field(k, carry):
            lanes = pl.ds(pl.multiple_of(k * 1024, 1024), 1024)
            t = dot(s_buf[...], vp_all[k].reshape(1024, 512), NT)
            t = (t[:96] + t[96:]) * u_own[:, lanes].astype(F32)
            t = jnp.sum(t, axis=0, keepdims=True)
            for n in range(8):
                part_out[k * 8 + n] = jnp.broadcast_to(t[:, n * 128 : (n + 1) * 128], (8, 128))
            return carry

        lax.fori_loop(0, 4, field, 0)
        t = dot(s_buf[...], up_all[...].reshape(512, 512), NT)
        t = jnp.sum((t[:96] + t[96:]) * v_own[...].astype(F32), axis=0, keepdims=True)
        for n in range(NR):
            part4_out[n] = jnp.broadcast_to(t[:, n * 128 : (n + 1) * 128], (8, 128))

        def part_send(r, carry):
            o = lax.rem(j + r, NC)
            send(part_out.at[o, pl.ds(0, 1)], part_in.at[j, pl.ds(0, 1)], 14, line(r))
            return carry

        lax.fori_loop(1, NC, part_send, 0)
        for r in range(1, NR):
            o = lax.rem(i + r, NR)
            send(part4_out.at[o, pl.ds(0, 1)], part4_in.at[i, pl.ds(0, 1)], 15, file(r))
        part_in[j] = part_out[j]
        part4_in[i] = part4_out[i]

        tot[...] = jnp.zeros((512, 256), F32)

        def blocks(b, carry):
            a = at[b].astype(F32)
            right = bt[b]
            hi, lo = pieces2(a * c_l[b][:1])
            half_t = dot(hi, right, NT) + dot(lo, right, NT)
            w = sym[b] * (half_t + half_t.T)
            hi, lo = pieces2(w)
            mixed = dot(hi, right) + dot(lo, right)
            values = 2.0 * jnp.sum(a * mixed, axis=0, keepdims=True)
            tot[...] += spread(values, tall_l[b], wide_l[b])
            return carry

        lax.fori_loop(0, 4, blocks, 0)

        got(k_in.at[pl.ds(0, ND - 1)], 13)
        k_red[...] = jnp.sum(k_in[...].astype(F32), axis=0).astype(BF)
        everyone(lambda o, where: send(k_red, k_full.at[k_rows, k_lanes], 16, where))
        k_full[k_rows, k_lanes] = k_red[...]
        lax.fori_loop(4, 8, blocks, 0)

        got(k_in.at[pl.ds(0, ND - 1)], 16)
        gone(k_in.at[pl.ds(0, ND - 1)], 13)
        gone(k_in.at[pl.ds(0, ND - 1)], 16)
        hi, lo = pieces2(k_full[...].astype(F32) * quad[...])
        y = dot(vp_all[x, core, z], hi) + dot(vp_all[x, core, z], lo)
        y = y * up_all[i].astype(F32)
        y = y[:, :128] + y[:, 128:256] + y[:, 256:384] + y[:, 384:]
        y = jnp.sum(y.T, axis=0, keepdims=True)
        got(part_in.at[pl.ds(0, NC - 1), pl.ds(0, 1)], 14)
        got(part4_in.at[pl.ds(0, NR - 1), pl.ds(0, 1)], 15)
        gone(part_in.at[pl.ds(0, NC - 1), pl.ds(0, 1)], 14)
        gone(part4_in.at[pl.ds(0, NR - 1), pl.ds(0, 1)], 15)
        parts = jnp.sum(part_in[:, :1, :], axis=0) + jnp.sum(part4_in[:, :1, :], axis=0)
        tot[...] += spread(2.0 * (y + parts), tall_t[...], wide_t[...])

        def t_send(o, where):
            rows, lanes = place(o)
            send(tot.at[rows, lanes], t_in.at[me], 17, where)

        everyone(t_send)
        t_in[me] = tot[my_rows, my_lanes]
        rr = rr_buf[...]

        @pl.when(it < ITERS - 1)
        def _():
            got(t_in.at[pl.ds(0, ND - 1)], 17)
            t_red[...] = jnp.sum(t_in[...], axis=0)
            everyone(lambda o, where: send(t_red, full.at[my_rows, my_lanes], 18, where))
            full[my_rows, my_lanes] = t_red[...]
            gone(t_in.at[pl.ds(0, ND - 1)], 17)
            got(t_in.at[pl.ds(0, ND - 1)], 18)
            gone(t_in.at[pl.ds(0, ND - 1)], 18)

            direction = vec[...]
            applied = direction + full[...]
            step = rr / jnp.broadcast_to(jnp.sum(direction * applied, keepdims=True), (8, 128))
            res = ret[...] - step[:1, :1] * applied
            ret[...] = res
            new = jnp.broadcast_to(jnp.sum(res * res, keepdims=True), (8, 128))
            beta = new / rr
            vec[...] = res + beta[:1, :1] * direction
            rr_buf[...] = new
            spread_c()
            out[0] += step * dir_own[...]
            out[1] -= step * (dir_own[...] + t_red[...])
            dir_own[...] = out[1] + beta * dir_own[...]
            lax.fori_loop(0, 8, take, 0)

        @pl.when(it == ITERS - 1)
        def _():
            direction = vec[...]
            share = jnp.broadcast_to(jnp.sum(tot[...] * direction, keepdims=True), (8, 128))
            s_out[...] = share
            s_in[me] = share
            row0 = pl.ds(0, 1)
            everyone(lambda o, where: send(s_out.at[row0], s_in.at[me, row0], 18, where))
            got(t_in.at[pl.ds(0, ND - 1)], 17)
            got(s_in.at[pl.ds(0, ND - 1), row0], 18)
            whole = jnp.sum(s_in[:, :1, :], axis=0) + jnp.sum(direction * direction, keepdims=True)
            step = rr[:1] / whole
            out[0] += step * dir_own[...]
            out[1] -= step * (dir_own[...] + jnp.sum(t_in[...], axis=0))
            gone(t_in.at[pl.ds(0, ND - 1)], 17)
            gone(s_in.at[pl.ds(0, ND - 1), row0], 18)

        return carry

    lax.fori_loop(0, ITERS, iterate, 0)

    gone(p_cols.at[pl.ds(0, 3)], 0)
    gone(v_own.at[:, pl.ds(0, 384)], 1)
    gone(u_own.at[:, pl.ds(0, 31 * 128)], 2)
    gone(t_in.at[pl.ds(0, ND - 1)], 3)
    gone(p_rows.at[:, 0], 4)
    gone(p_rows.at[pl.ds(0, 3), 0, 0], 5)
    gone(p_rows.at[:, 0, pl.ds(0, 3)], 6)
    gone(vp_all.at[:, 0], 7)
    gone(vp_all.at[pl.ds(0, 3), 0, 0], 8)
    gone(vp_all.at[:, 0, pl.ds(0, 3)], 9)
    gone(up_all.at[pl.ds(0, 3)], 10)

    @pl.when(moved)
    def _():
        gone(p_cols.at[0], 19)
        gone(v_own.at[:, pl.ds(0, 128)], 20)
        gone(v_tile, 21)
        gone(own_t, 22)
        gone(u_tile, 23)
        gone(u_own.at[:, pl.ds(0, 128)], 24)


def local(
    right_side, eigen_basis, tile_left, tile_right, piece_owner, omega_main, damping,
    local_basis, local_omega, local_left, local_right, local_owner,
):
    vmem = pl.BlockSpec(memory_space=pltpu.VMEM)
    V = pltpu.VMEM
    far = pl.BlockSpec(memory_space=pl.ANY)
    scratch = [
        V((8, 256, 256), BF),
        V((8, 256, 256), F32),
        V((8, 256, 256), BF),
        V((8, 256, 256), BF),
        V((4, 96, 128), BF),
        V((4, 96, 128), BF),
        V((32, 96, 128), BF),
        V((1, 128), jnp.int32),
        V((4, 2, 4, 96, 512), BF),
        V((4, 96, 512), BF),
        V((96, 4096), BF),
        V((96, 512), BF),
        V((4, 2, 4, 128, 512), BF),
        V((4, 128, 512), BF),
        V((8, 256, 256), BF),
        V((8, 256, 256), BF),
        V((8, 256, 256), F32),
        V((8, 512, 256), BF),
        V((8, 256, 256), BF),
        V((512, 128), BF),
        V((256, 128), BF),
        V((512, 512), F32),
        V((512, 256), F32),
        V((512, 256), F32),
        V((512, 256), F32),
        V((1536, 256), BF),
        V((8, 8, 256), F32),
        V((32, 8, 128), F32),
        V((4, 8, 128), F32),
        V((32, 8, 128), F32),
        V((32, 8, 128), F32),
        V((4, 8, 128), F32),
        V((4, 8, 128), F32),
        V((192, 512), BF),
        V((512, 512), BF),
        V((128, 16, 128), BF),
        V((16, 128), BF),
        V((512, 512), BF),
        V((512, 256), F32),
        V((128, 8, 128), F32),
        V((8, 128), F32),
        V((8, 128), F32),
        V((128, 8, 128), F32),
        V((8, 128), F32),
        V((8, 128), F32),
        pltpu.SemaphoreType.DMA((25,)),
        pltpu.SemaphoreType.DMA((25,)),
        pltpu.SemaphoreType.DMA((6,)),
    ]
    out = pl.pallas_call(
        kernel,
        out_shape=jax.ShapeDtypeStruct((2, 8, 128), F32),
        in_specs=[vmem, vmem, far] + [vmem] * 5 + [far] * 4,
        out_specs=vmem,
        scratch_shapes=scratch,
        name="newton",
        compiler_params=pltpu.CompilerParams(
            collective_id=0, has_side_effects=True, vmem_limit_bytes=56 * 1024 * 1024
        ),
    )(
        right_side.reshape(8, 128),
        eigen_basis,
        tile_left.reshape(32, 96, 128),
        tile_right,
        piece_owner,
        local_owner,
        omega_main,
        damping.reshape(1, 512),
        local_basis,
        local_omega,
        local_left,
        local_right,
    )
    both = out.reshape(2, 1024)
    return both[0], both[1]


def solution(mesh):
    both = ("row", "col")
    placed = (
        P(both), P(both, None), P("row", "col"), P("row", "col"), P("row", "col"), P(), P(),
        P(both, None, None), P(both, None, None), P(both, None, None), P(both, None, None),
        P(both, None),
    )
    return jax.shard_map(
        local, mesh=mesh, in_specs=placed, out_specs=(P(both), P(both)), check_vma=False
    )
```

time: 200 us -> 157 us (0.79)
  Pallas kernels: 193 us -> 155 us
  local copies, waits for them, and re-layouts: 5.7 us -> 1.28 us
    pallas_call x1, Pallas kernels: 193 us -> 155 us  [local(): pl.pallas_call(kernel, out_shape=jax.ShapeDtypeStruct((2, 8, 128), F32),...]
    unnamed x2 -> x0, local copies, waits for them, and re-layouts: 2.54 us -> none
where the time goes in v2:
time: 157 us
  Pallas kernels  155 us (99%)
    pallas_call x1, Pallas kernels, local(): pl.pallas_call(kernel, out_shape=jax.ShapeDtypeStruct((2, 8, 128), F32),...  155 us

profile of v2, /device:TPU:1, one launch (start us, length us, event | category | flops | bytes accessed | tf_op | source)
XLA Modules:
  0.0 157.1 jit_solution(6836015238067567371)
XLA Ops:
  0.6 155.2 %newton.1 = f32[2,8,128]{2,1,0:T(8,128)} custom-call(f32[8,128]{1,0:T(8,128)} %bitcast.8, bf16[96,512]{1,0:T(8,128)(2,1)} %p_own.1, bf16[32,96,128]{2,1,0:T(8,128)(2,1)} %bitcast.7, bf16[128,384]{1,0:T(8,128)(2,1)} %v_raw.1, s32[1,128]{1,0:T(1,128)} %own_in.1, s32[8,256]{1,0:T(8,128)} %own_l.1, f32[512,512]{1,0:T(8,128)} %omega.1, f32[1,512]{1,0:T(1,128)} %bitcast.9, ...), custom_call_target="tpu_custom_call" | custom-call | tf_op jit(solution)/shard_map/newton/pallas_call | solution.py:542
  155.8 1.3 slice_bitcast_fusion

commit v3 on v2

--- a/solution.py
+++ b/solution.py
@@ -32,16 +32,17 @@
     return hi, mid, (rest - mid.astype(F32)).astype(BF)
 
 
-def place(q):
-    rows = pl.ds(pl.multiple_of(lax.rem(q, 64) * 8, 8), 8)
-    lanes = pl.ds(pl.multiple_of((q // 64) * 128, 128), 128)
-    return rows, lanes
-
-
-def spot(q):
-    rows = pl.ds(pl.multiple_of((q // 4) * 16, 16), 16)
-    lanes = pl.ds(pl.multiple_of(lax.rem(q, 4) * 128, 128), 128)
-    return rows, lanes
+class Place:
+    def __init__(self, x, h, z, low, core):
+        self.where = (low * 2 + core, x * 8 + h * 4 + z)
+        self.chunk = (
+            pl.ds(pl.multiple_of(core * 256 + x * 64 + h * 32 + z * 8, 8), 8),
+            pl.ds(pl.multiple_of(low * 128, 128), 128),
+        )
+        self.block = (
+            pl.ds(pl.multiple_of(low * 256 + core * 128 + x * 32 + h * 16, 16), 16),
+            pl.ds(pl.multiple_of(z * 128, 128), 128),
+        )
 
 
 def hots(owner):
@@ -70,7 +71,7 @@
     out,
     l_basis, l_omega, l_left, l_right, v_in, v_tile, u_tile, own_t,
     p_rows, p_cols, u_own, v_own, vp_all, up_all, at, bt, sym, tall_l, wide_l, tall_t, wide_t,
-    quad, full, vec, ret, d3, c_l, c_col, c_row, part_out, part_in, part4_out, part4_in,
+    quad, full, vec, ret, d3, c_l, c_me, c_col, c_row, part_out, part_in, part4_out, part4_in,
     s_buf, k_out, k_in, k_red, k_full, tot, t_in, t_red, s_out, s_in, dir_own, rr_buf,
     ssem, rsem, lsem,
 ):
@@ -92,9 +93,6 @@
             (jj // 8) * 8 + lax.rem(ii, 2) * 4 + lax.rem(jj, 4),
         )
 
-    def line(r):
-        return holder(i, lax.rem(j + r, NC))
-
     def file(r):
         return holder(lax.rem(i + r, NR), j)
 
@@ -114,13 +112,38 @@
     def gone(ref, k):
         pltpu.make_async_copy(ref, ref, ssem.at[k]).wait()
 
+    ahead = (2, 3, 1, 0)
+    y = h * 2 + row // 2
+    zs = [lax.rem(z + k, 4) for k in ahead]
+    ys = [lax.rem(y + k, 4) for k in ahead]
+    ys = [(lax.rem(k, 2), k // 2) for k in ys]
+
+    def far(k):
+        return lax.rem(x + 2 + (k * (k + 1)) // 2, 4)
+
+    def spots(count, inner, body):
+        def step(k, carry):
+            for at_inner in inner:
+                body(k, *at_inner)
+            return carry
+
+        lax.fori_loop(0, count - 1, step, 0)
+        for at_inner in inner[:-1]:
+            body(count - 1, *at_inner)
+
     def everyone(body):
-        def step(r, carry):
-            o = lax.rem(me + r, ND)
-            body(o, (o // NC, lax.rem(o, NC)))
-            return carry
-
-        lax.fori_loop(1, ND, step, 0)
+        inner = [(zz, yy) for zz in zs for yy in ys]
+
+        def one(k, zz, yy):
+            cc = lax.rem(core + 1 - k // 4, 2)
+            body(Place(far(lax.rem(k, 4)), yy[1], zz, yy[0], cc))
+
+        spots(8, inner, one)
+
+    def plane(body):
+        inner = [(cc, zz) for cc in (1 - core, core) for zz in zs]
+        low = row // 2
+        spots(4, inner, lambda k, cc, zz: body(far(k) * 8 + cc * 4 + zz, Place(far(k), h, zz, low, cc).where))
 
     loads = [
         pltpu.make_async_copy(src, dst, lsem.at[n])
@@ -130,25 +153,26 @@
     ]
     for load in loads:
         load.start()
-    v_in[...] = v_raw[...].astype(F32).T.astype(BF).reshape(4, 96, 128)
-
     barrier = pltpu.get_barrier_semaphore()
     everyone(
-        lambda o, where: pl.semaphore_signal(
-            barrier, inc=1, device_id=where, device_id_type=MESH
-        )
+        lambda o: pl.semaphore_signal(barrier, inc=1, device_id=o.where, device_id_type=MESH)
     )
+    v_in[...] = v_raw[...].astype(F32).T.astype(BF).reshape(4, 96, 128)
     pl.semaphore_wait(barrier, ND - 1)
 
     lane_row = pl.ds(pl.multiple_of(row * 128, 128), 128)
     lane_col = pl.ds(pl.multiple_of(col * 128, 128), 128)
+
+    @pl.when(moved)
+    def _():
+        send(p_own, p_cols.at[row], 19, holder(row, col))
+
     for r in range(1, NR):
         o = lax.rem(row + r, NR)
         send(p_own, p_cols.at[row], 0, holder(o, col))
 
     @pl.when(moved)
     def _():
-        send(p_own, p_cols.at[row], 19, holder(row, col))
         send(v_in, v_tile, 21, holder(row, col))
         send(own_in, own_t, 22, holder(row, col))
 
@@ -158,64 +182,10 @@
         v_tile[...] = v_in[...]
         own_t[...] = own_in[...]
 
-    got(p_cols.at[pl.ds(0, 3)], 0)
-
-    @pl.when(moved)
-    def _():
-        got(p_cols.at[0], 19)
-        got(v_tile, 21)
-        got(own_t, 22)
-
-    A, B = pl.ds(0, 48), pl.ds(48, 48)
-    for r in (1, 3, 2):
-        send(p_cols.at[i, A], p_rows.at[x, core, z, A], 5, dev(x, lax.rem(z + r, 4)))
-        send(p_cols.at[i, B], p_rows.at[x, core, z, B], 5, dev(lax.rem(x + r, 4), z))
-    p_rows[x, core, z] = p_cols[i]
-
-    vp = dot(v_tile[...].reshape(384, 128), p_cols[...].reshape(384, 512), TN).astype(BF)
-    vp_all[x, core, z] = vp
-
-    my_rows, my_lanes = place(me)
-    everyone(lambda o, where: send(rhs, vec.at[my_rows, my_lanes], 3, where))
+    own = Place(x, h, z, row // 2, core)
+    my_rows, my_lanes = own.chunk
+    everyone(lambda o: send(rhs, vec.at[my_rows, my_lanes], 3, o.where))
     vec[my_rows, my_lanes] = rhs[...]
-
-    got(p_rows.at[pl.ds(0, 3), 0, 0], 5)
-    for r in (1, 3, 2):
-        send(p_rows.at[x, core, :, A], p_rows.at[x, core, :, A], 6, dev(lax.rem(x + r, 4), z))
-        send(p_rows.at[:, core, z, B], p_rows.at[:, core, z, B], 6, dev(x, lax.rem(z + r, 4)))
-
-    @pl.when(moved)
-    def _():
-        send(u_in, u_tile, 23, holder(row, col))
-
-    @pl.when(kept)
-    def _():
-        pltpu.make_async_copy(u_in, u_tile, lsem.at[4]).start()
-
-    C, D = pl.ds(0, 64), pl.ds(64, 64)
-    for r in (1, 3, 2):
-        send(vp_all.at[x, core, z, C], vp_all.at[x, core, z, C], 8, dev(x, lax.rem(z + r, 4)))
-        send(vp_all.at[x, core, z, D], vp_all.at[x, core, z, D], 8, dev(lax.rem(x + r, 4), z))
-    for r in range(1, NR):
-        o = lax.rem(row + r, NR)
-        send(v_in.at[o], v_own.at[:, lane_row], 1, holder(o, col))
-
-    def u_send(r, carry):
-        o = lax.rem(col + r, NC)
-        send(u_in.at[o], u_own.at[:, lane_col], 2, holder(row, o))
-        return carry
-
-    lax.fori_loop(1, NC, u_send, 0)
-
-    @pl.when(moved)
-    def _():
-        send(v_in.at[row], v_own.at[:, lane_row], 20, holder(row, col))
-        send(u_in.at[col], u_own.at[:, lane_col], 24, holder(row, col))
-
-    @pl.when(kept)
-    def _():
-        v_own[:, lane_row] = v_in[row]
-        pltpu.make_async_copy(u_in.at[col], u_own.at[:, lane_col], lsem.at[5]).start()
 
     def prepare(b, carry):
         basis = l_basis[b]
@@ -228,37 +198,127 @@
         wide_l[b] = wide
         return carry
 
+    for load in loads:
+        load.wait()
+    lax.fori_loop(0, 6, prepare, 0)
+
+    @pl.when(moved)
+    def _():
+        got(p_cols.at[0], 19)
+
+    A, B = pl.ds(0, 48), pl.ds(48, 48)
+    for r in (1, 3, 2):
+        send(p_cols.at[i, A], p_rows.at[x, core, z, A], 5, dev(x, lax.rem(z + r, 4)))
+        send(p_cols.at[i, B], p_rows.at[x, core, z, B], 5, dev(lax.rem(x + r, 4), z))
+    p_rows[x, core, z] = p_cols[i]
+
+    got(p_cols.at[pl.ds(0, 3)], 0)
+
+    @pl.when(moved)
+    def _():
+        got(v_tile, 21)
+        got(own_t, 22)
+
+    vp = dot(v_tile[...].reshape(384, 128), p_cols[...].reshape(384, 512), TN).astype(BF)
+    vp_all[x, core, z] = vp
+    C, D = pl.ds(0, 64), pl.ds(64, 64)
+    for r in (1, 3, 2):
+        send(vp_all.at[x, core, z, C], vp_all.at[x, core, z, C], 8, dev(x, lax.rem(z + r, 4)))
+        send(vp_all.at[x, core, z, D], vp_all.at[x, core, z, D], 8, dev(lax.rem(x + r, 4), z))
+
+    @pl.when(moved)
+    def _():
+        send(u_in, u_tile, 23, holder(row, col))
+
+    @pl.when(kept)
+    def _():
+        pltpu.make_async_copy(u_in, u_tile, lsem.at[4]).start()
+
+    got(p_rows.at[pl.ds(0, 3), 0, 0], 5)
+    for r in (1, 3, 2):
+        send(p_rows.at[x, core, :, A], p_rows.at[x, core, :, A], 6, dev(lax.rem(x + r, 4), z))
+        send(p_rows.at[:, core, z, B], p_rows.at[:, core, z, B], 6, dev(x, lax.rem(z + r, 4)))
+
     tall, wide = hots(own_t[...])
     tall_t[...] = tall
     wide_t[...] = wide
-    for load in loads:
-        load.wait()
-
-    def spread_c():
-        d3[...] = jnp.concatenate(pieces3(vec[...]), axis=0)
-        c_own = jnp.broadcast_to(fetch(d3[...], tall_t[...], wide_t[...]), (8, 128))
-        c_col[j] = c_own
-        c_row[i] = c_own
-
-        def c_send(r, carry):
-            send(c_col.at[j, pl.ds(0, 1)], c_col.at[j, pl.ds(0, 1)], 11, line(r))
-            return carry
-
-        lax.fori_loop(1, NC, c_send, 0)
-        for r in range(1, NR):
-            send(c_row.at[i, pl.ds(0, 1)], c_row.at[i, pl.ds(0, 1)], 12, file(r))
-
-    def take(b, carry):
-        c_l[b] = jnp.broadcast_to(fetch(d3[...], tall_l[b], wide_l[b]), (8, 256))
-        return carry
-
-    lax.fori_loop(0, 2, prepare, 0)
+
     got(vp_all.at[pl.ds(0, 3), 0, 0], 8)
     for r in (1, 3, 2):
         send(vp_all.at[x, core, :, C], vp_all.at[x, core, :, C], 9, dev(lax.rem(x + r, 4), z))
         send(vp_all.at[:, core, z, D], vp_all.at[:, core, z, D], 9, dev(x, lax.rem(z + r, 4)))
-    got(p_rows.at[:, 0, pl.ds(0, 3)], 6)
-    send(p_rows.at[:, core], p_rows.at[:, core], 4, sibling)
+
+    def u_send(k, hh, zz):
+        xx = far(k)
+        there = ((row // 2) * 2 + hh, xx * 8 + core * 4 + zz)
+        send(u_in.at[xx * 8 + hh * 4 + zz], u_own.at[:, lane_col], 2, there)
+
+    spots(4, [(hh, zz) for hh in (1 - h, h) for zz in zs], u_send)
+    for r in range(1, NR):
+        o = lax.rem(row + r, NR)
+        send(v_in.at[o], v_own.at[:, lane_row], 1, holder(o, col))
+
+    @pl.when(moved)
+    def _():
+        send(v_in.at[row], v_own.at[:, lane_row], 20, holder(row, col))
+        send(u_in.at[col], u_own.at[:, lane_col], 24, holder(row, col))
+
+    @pl.when(kept)
+    def _():
+        v_own[:, lane_row] = v_in[row]
+        pltpu.make_async_copy(u_in.at[col], u_own.at[:, lane_col], lsem.at[5]).start()
+
+
+    def spread_c():
+        d3[...] = jnp.concatenate(pieces3(vec[...]), axis=0)
+        c_own = jnp.broadcast_to(fetch(d3[...], tall_t[...], wide_t[...]), (8, 128))
+        c_me[...] = c_own
+        c_col[j] = c_own
+        c_row[i] = c_own
+
+        plane(lambda jj, where: send(c_me.at[pl.ds(0, 1)], c_col.at[j, pl.ds(0, 1)], 11, where))
+        for r in range(1, NR):
+            send(c_me.at[pl.ds(0, 1)], c_row.at[i, pl.ds(0, 1)], 12, file(r))
+
+    def take(b, carry):
+        c_l[b] = jnp.broadcast_to(fetch(d3[...], tall_l[b], wide_l[b]), (8, 256))
+        return carry
+
+    k_rows, k_lanes = own.block
+
+    def start_k():
+        c = jnp.broadcast_to(c_me[...][:1], (128, 128)).T
+        c = jnp.concatenate([c] * 4, axis=1)
+        vp = vp_all[x, core, z]
+        up = up_all[i]
+        sv = (vp.astype(F32) * c).astype(BF)
+        su = (up.astype(F32) * c).astype(BF)
+        k_out[...] = (dot(up, sv, TN) + dot(vp, su, TN)).astype(BF)
+
+        def k_send(o):
+            rows, lanes = o.block
+            send(k_out.at[rows, lanes], k_in.at[me], 13, o.where)
+
+        everyone(k_send)
+        k_in[me] = k_out[k_rows, k_lanes]
+
+    def turn_k():
+        got(k_in.at[pl.ds(0, ND - 1)], 13)
+        k_red[...] = jnp.sum(k_in[...].astype(F32), axis=0).astype(BF)
+        everyone(lambda o: send(k_red, k_full.at[k_rows, k_lanes], 16, o.where))
+        k_full[k_rows, k_lanes] = k_red[...]
+
+    def blocks(b, carry):
+        a = at[b].astype(F32)
+        right = bt[b]
+        hi, lo = pieces2(a * c_l[b][:1])
+        half_t = dot(hi, right, NT) + dot(lo, right, NT)
+        w = sym[b] * (half_t + half_t.T)
+        hi, lo = pieces2(w)
+        mixed = dot(hi, right) + dot(lo, right)
+        values = 2.0 * jnp.sum(a * mixed, axis=0, keepdims=True)
+        tot[...] += spread(values, tall_l[b], wide_l[b])
+        return carry
 
     got(t_in.at[pl.ds(0, ND - 1)], 3)
     first = vec[...]
@@ -268,17 +328,20 @@
     out[0] = jnp.zeros_like(rhs)
     rr_buf[...] = jnp.broadcast_to(jnp.sum(first * first, keepdims=True), (8, 128))
     spread_c()
-    lax.fori_loop(2, 5, prepare, 0)
+    lax.fori_loop(6, 8, prepare, 0)
+    lax.fori_loop(0, 8, take, 0)
+    got(p_rows.at[:, 0, pl.ds(0, 3)], 6)
+    send(p_rows.at[:, core], p_rows.at[:, core], 4, sibling)
+
+    @pl.when(moved)
+    def _():
+        got(u_tile, 23)
+
+    @pl.when(kept)
+    def _():
+        pltpu.make_async_copy(u_in, u_tile, lsem.at[4]).wait()
 
     got(p_rows.at[:, 0], 4)
-
-    @pl.when(moved)
-    def _():
-        got(u_tile, 23)
-
-    @pl.when(kept)
-    def _():
-        pltpu.make_async_copy(u_in, u_tile, lsem.at[4]).wait()
 
     def project(k, acc):
         u = u_tile[pl.ds(k * 8, 8)].reshape(768, 128)
@@ -288,13 +351,16 @@
     up_all[i] = up
     for r in range(1, NR):
         send(up_all.at[i], up_all.at[i], 10, file(r))
+    start_k()
 
     got(vp_all.at[:, 0, pl.ds(0, 3)], 9)
     send(vp_all.at[:, core], vp_all.at[:, core], 7, sibling)
-    lax.fori_loop(5, 8, prepare, 0)
+    tot[...] = jnp.zeros((512, 256), F32)
+    lax.fori_loop(0, 6, blocks, 0)
     t = 0.5 * omega[...] - damp[...]
     quad[...] = t + t.T
-    lax.fori_loop(0, 8, take, 0)
+    turn_k()
+    lax.fori_loop(6, 8, blocks, 0)
 
     got(u_own.at[:, pl.ds(0, 31 * 128)], 2)
     got(v_own.at[:, pl.ds(0, 384)], 1)
@@ -330,15 +396,6 @@
         su = [(up_all[n].astype(F32) * c[:, n : n + 1]).astype(BF) for n in range(NR)]
         s = lax.fori_loop(0, 4, add_rows, dot(v_own[...], jnp.concatenate(su, axis=0)))
         s = s.astype(BF)
-        k_out[...] = dot(p_cols[i], s, TN).astype(BF)
-
-        def k_send(o, where):
-            rows, lanes = spot(o)
-            send(k_out.at[rows, lanes], k_in.at[me], 13, where)
-
-        everyone(k_send)
-        k_rows, k_lanes = spot(me)
-        k_in[me] = k_out[k_rows, k_lanes]
 
         s_buf[...] = jnp.concatenate(pieces2(s.astype(F32) * damp[...]), axis=0)
 
@@ -357,39 +414,22 @@
         for n in range(NR):
             part4_out[n] = jnp.broadcast_to(t[:, n * 128 : (n + 1) * 128], (8, 128))
 
-        def part_send(r, carry):
-            o = lax.rem(j + r, NC)
-            send(part_out.at[o, pl.ds(0, 1)], part_in.at[j, pl.ds(0, 1)], 14, line(r))
-            return carry
-
-        lax.fori_loop(1, NC, part_send, 0)
+        plane(
+            lambda jj, where: send(
+                part_out.at[jj, pl.ds(0, 1)], part_in.at[j, pl.ds(0, 1)], 14, where
+            )
+        )
         for r in range(1, NR):
             o = lax.rem(i + r, NR)
             send(part4_out.at[o, pl.ds(0, 1)], part4_in.at[i, pl.ds(0, 1)], 15, file(r))
         part_in[j] = part_out[j]
         part4_in[i] = part4_out[i]
 
-        tot[...] = jnp.zeros((512, 256), F32)
-
-        def blocks(b, carry):
-            a = at[b].astype(F32)
-            right = bt[b]
-            hi, lo = pieces2(a * c_l[b][:1])
-            half_t = dot(hi, right, NT) + dot(lo, right, NT)
-            w = sym[b] * (half_t + half_t.T)
-            hi, lo = pieces2(w)
-            mixed = dot(hi, right) + dot(lo, right)
-            values = 2.0 * jnp.sum(a * mixed, axis=0, keepdims=True)
-            tot[...] += spread(values, tall_l[b], wide_l[b])
-            return carry
-
-        lax.fori_loop(0, 4, blocks, 0)
-
-        got(k_in.at[pl.ds(0, ND - 1)], 13)
-        k_red[...] = jnp.sum(k_in[...].astype(F32), axis=0).astype(BF)
-        everyone(lambda o, where: send(k_red, k_full.at[k_rows, k_lanes], 16, where))
-        k_full[k_rows, k_lanes] = k_red[...]
-        lax.fori_loop(4, 8, blocks, 0)
+        @pl.when(it > 0)
+        def _():
+            turn_k()
+            tot[...] = jnp.zeros((512, 256), F32)
+            lax.fori_loop(0, 8, blocks, 0)
 
         got(k_in.at[pl.ds(0, ND - 1)], 16)
         gone(k_in.at[pl.ds(0, ND - 1)], 13)
@@ -406,9 +446,9 @@
         parts = jnp.sum(part_in[:, :1, :], axis=0) + jnp.sum(part4_in[:, :1, :], axis=0)
         tot[...] += spread(2.0 * (y + parts), tall_t[...], wide_t[...])
 
-        def t_send(o, where):
-            rows, lanes = place(o)
-            send(tot.at[rows, lanes], t_in.at[me], 17, where)
+        def t_send(o):
+            rows, lanes = o.chunk
+            send(tot.at[rows, lanes], t_in.at[me], 17, o.where)
 
         everyone(t_send)
         t_in[me] = tot[my_rows, my_lanes]
@@ -418,7 +458,7 @@
         def _():
             got(t_in.at[pl.ds(0, ND - 1)], 17)
             t_red[...] = jnp.sum(t_in[...], axis=0)
-            everyone(lambda o, where: send(t_red, full.at[my_rows, my_lanes], 18, where))
+            everyone(lambda o: send(t_red, full.at[my_rows, my_lanes], 18, o.where))
             full[my_rows, my_lanes] = t_red[...]
             gone(t_in.at[pl.ds(0, ND - 1)], 17)
             got(t_in.at[pl.ds(0, ND - 1)], 18)
@@ -434,6 +474,7 @@
             vec[...] = res + beta[:1, :1] * direction
             rr_buf[...] = new
             spread_c()
+            start_k()
             out[0] += step * dir_own[...]
             out[1] -= step * (dir_own[...] + t_red[...])
             dir_own[...] = out[1] + beta * dir_own[...]
@@ -446,7 +487,7 @@
             s_out[...] = share
             s_in[me] = share
             row0 = pl.ds(0, 1)
-            everyone(lambda o, where: send(s_out.at[row0], s_in.at[me, row0], 18, where))
+            everyone(lambda o: send(s_out.at[row0], s_in.at[me, row0], 18, o.where))
             got(t_in.at[pl.ds(0, ND - 1)], 17)
             got(s_in.at[pl.ds(0, ND - 1), row0], 18)
             whole = jnp.sum(s_in[:, :1, :], axis=0) + jnp.sum(direction * direction, keepdims=True)
@@ -517,6 +558,7 @@
         V((512, 256), F32),
         V((1536, 256), BF),
         V((8, 8, 256), F32),
+        V((8, 128), F32),
         V((32, 8, 128), F32),
         V((4, 8, 128), F32),
         V((32, 8, 128), F32),

time: 157 us -> 132 us (0.84)
  Pallas kernels: 155 us -> 130 us
    pallas_call x1, Pallas kernels: 155 us -> 130 us  [local(): pl.pallas_call(kernel, out_shape=jax.ShapeDtypeStruct((2, 8, 128), F32),...]
where the time goes in v3:
time: 132 us
  Pallas kernels  130 us (98%)
    pallas_call x1, Pallas kernels, local(): pl.pallas_call(kernel, out_shape=jax.ShapeDtypeStruct((2, 8, 128), F32),...  130 us

profile of v3, /device:TPU:1, one launch (start us, length us, event | category | flops | bytes accessed | tf_op | source)
XLA Modules:
  0.0 132.3 jit_solution(14416431091990689886)
XLA Ops:
  0.6 130.3 %newton.1 = f32[2,8,128]{2,1,0:T(8,128)} custom-call(f32[8,128]{1,0:T(8,128)} %bitcast.8, bf16[96,512]{1,0:T(8,128)(2,1)} %p_own.1, bf16[32,96,128]{2,1,0:T(8,128)(2,1)} %bitcast.7, bf16[128,384]{1,0:T(8,128)(2,1)} %v_raw.1, s32[1,128]{1,0:T(1,128)} %own_in.1, s32[8,256]{1,0:T(8,128)} %own_l.1, f32[512,512]{1,0:T(8,128)} %omega.1, f32[1,512]{1,0:T(1,128)} %bitcast.9, ...), custom_call_target="tpu_custom_call" | custom-call | tf_op jit(solution)/shard_map/newton/pallas_call | solution.py:584
  131.0 1.3 slice_bitcast_fusion

commit v4 on v3

--- a/solution.py
+++ b/solution.py
@@ -201,6 +201,8 @@
     for load in loads:
         load.wait()
     lax.fori_loop(0, 6, prepare, 0)
+    t = 0.5 * omega[...] - damp[...]
+    quad[...] = t + t.T
 
     @pl.when(moved)
     def _():
@@ -269,13 +271,14 @@
         pltpu.make_async_copy(u_in.at[col], u_own.at[:, lane_col], lsem.at[5]).start()
 
 
-    def spread_c():
+    def find_c():
         d3[...] = jnp.concatenate(pieces3(vec[...]), axis=0)
         c_own = jnp.broadcast_to(fetch(d3[...], tall_t[...], wide_t[...]), (8, 128))
         c_me[...] = c_own
         c_col[j] = c_own
         c_row[i] = c_own
 
+    def spread_c():
         plane(lambda jj, where: send(c_me.at[pl.ds(0, 1)], c_col.at[j, pl.ds(0, 1)], 11, where))
         for r in range(1, NR):
             send(c_me.at[pl.ds(0, 1)], c_row.at[i, pl.ds(0, 1)], 12, file(r))
@@ -327,11 +330,12 @@
     out[1] = rhs[...]
     out[0] = jnp.zeros_like(rhs)
     rr_buf[...] = jnp.broadcast_to(jnp.sum(first * first, keepdims=True), (8, 128))
+    find_c()
     spread_c()
     lax.fori_loop(6, 8, prepare, 0)
-    lax.fori_loop(0, 8, take, 0)
     got(p_rows.at[:, 0, pl.ds(0, 3)], 6)
     send(p_rows.at[:, core], p_rows.at[:, core], 4, sibling)
+    lax.fori_loop(0, 8, take, 0)
 
     @pl.when(moved)
     def _():
@@ -356,11 +360,8 @@
     got(vp_all.at[:, 0, pl.ds(0, 3)], 9)
     send(vp_all.at[:, core], vp_all.at[:, core], 7, sibling)
     tot[...] = jnp.zeros((512, 256), F32)
-    lax.fori_loop(0, 6, blocks, 0)
-    t = 0.5 * omega[...] - damp[...]
-    quad[...] = t + t.T
+    lax.fori_loop(0, 8, blocks, 0)
     turn_k()
-    lax.fori_loop(6, 8, blocks, 0)
 
     got(u_own.at[:, pl.ds(0, 31 * 128)], 2)
     got(v_own.at[:, pl.ds(0, 384)], 1)
@@ -473,8 +474,9 @@
             beta = new / rr
             vec[...] = res + beta[:1, :1] * direction
             rr_buf[...] = new
+            find_c()
+            start_k()
             spread_c()
-            start_k()
             out[0] += step * dir_own[...]
             out[1] -= step * (dir_own[...] + t_red[...])
             dir_own[...] = out[1] + beta * dir_own[...]

time: 132 us -> 136 us (1.030)
  Pallas kernels: 130 us -> 134 us
    pallas_call x1, Pallas kernels: 130 us -> 134 us  [local(): pl.pallas_call(kernel, out_shape=jax.ShapeDtypeStruct((2, 8, 128), F32),...]
where the time goes in v4:
time: 136 us
  Pallas kernels  134 us (99%)
    pallas_call x1, Pallas kernels, local(): pl.pallas_call(kernel, out_shape=jax.ShapeDtypeStruct((2, 8, 128), F32),...  134 us

profile of v4, /device:TPU:1, one launch (start us, length us, event | category | flops | bytes accessed | tf_op | source)
XLA Modules:
  0.0 135.9 jit_solution(13824426446597525711)
XLA Ops:
  0.6 134.0 %newton.1 = f32[2,8,128]{2,1,0:T(8,128)} custom-call(f32[8,128]{1,0:T(8,128)} %bitcast.8, bf16[96,512]{1,0:T(8,128)(2,1)} %p_own.1, bf16[32,96,128]{2,1,0:T(8,128)(2,1)} %bitcast.7, bf16[128,384]{1,0:T(8,128)(2,1)} %v_raw.1, s32[1,128]{1,0:T(1,128)} %own_in.1, s32[8,256]{1,0:T(8,128)} %own_l.1, f32[512,512]{1,0:T(8,128)} %omega.1, f32[1,512]{1,0:T(1,128)} %bitcast.9, ...), custom_call_target="tpu_custom_call" | custom-call | tf_op jit(solution)/shard_map/newton/pallas_call | solution.py:586
  134.6 1.3 slice_bitcast_fusion

commit v5 on v4

--- a/solution.py
+++ b/solution.py
@@ -271,14 +271,13 @@
         pltpu.make_async_copy(u_in.at[col], u_own.at[:, lane_col], lsem.at[5]).start()
 
 
-    def find_c():
+    def spread_c():
         d3[...] = jnp.concatenate(pieces3(vec[...]), axis=0)
         c_own = jnp.broadcast_to(fetch(d3[...], tall_t[...], wide_t[...]), (8, 128))
         c_me[...] = c_own
         c_col[j] = c_own
         c_row[i] = c_own
 
-    def spread_c():
         plane(lambda jj, where: send(c_me.at[pl.ds(0, 1)], c_col.at[j, pl.ds(0, 1)], 11, where))
         for r in range(1, NR):
             send(c_me.at[pl.ds(0, 1)], c_row.at[i, pl.ds(0, 1)], 12, file(r))
@@ -330,7 +329,6 @@
     out[1] = rhs[...]
     out[0] = jnp.zeros_like(rhs)
     rr_buf[...] = jnp.broadcast_to(jnp.sum(first * first, keepdims=True), (8, 128))
-    find_c()
     spread_c()
     lax.fori_loop(6, 8, prepare, 0)
     got(p_rows.at[:, 0, pl.ds(0, 3)], 6)
@@ -429,6 +427,7 @@
         @pl.when(it > 0)
         def _():
             turn_k()
+            lax.fori_loop(0, 8, take, 0)
             tot[...] = jnp.zeros((512, 256), F32)
             lax.fori_loop(0, 8, blocks, 0)
 
@@ -474,13 +473,11 @@
             beta = new / rr
             vec[...] = res + beta[:1, :1] * direction
             rr_buf[...] = new
-            find_c()
+            spread_c()
             start_k()
-            spread_c()
             out[0] += step * dir_own[...]
             out[1] -= step * (dir_own[...] + t_red[...])
             dir_own[...] = out[1] + beta * dir_own[...]
-            lax.fori_loop(0, 8, take, 0)
 
         @pl.when(it == ITERS - 1)
         def _():

time: 136 us -> 135 us (level)
  Pallas kernels: 134 us -> 132 us
    pallas_call x1, Pallas kernels: 134 us -> 132 us  [local(): pl.pallas_call(kernel, out_shape=jax.ShapeDtypeStruct((2, 8, 128), F32),...]
where the time goes in v5:
time: 135 us; the launch traced here: 134 us
  Pallas kernels  132 us (98%)
    pallas_call x1, Pallas kernels, local(): pl.pallas_call(kernel, out_shape=jax.ShapeDtypeStruct((2, 8, 128), F32),...  132 us

profile of v5, /device:TPU:1, one launch (start us, length us, event | category | flops | bytes accessed | tf_op | source)
XLA Modules:
  0.0 134.4 jit_solution(10194262733657994982)
XLA Ops:
  0.6 132.5 %newton.1 = f32[2,8,128]{2,1,0:T(8,128)} custom-call(f32[8,128]{1,0:T(8,128)} %bitcast.8, bf16[96,512]{1,0:T(8,128)(2,1)} %p_own.1, bf16[32,96,128]{2,1,0:T(8,128)(2,1)} %bitcast.7, bf16[128,384]{1,0:T(8,128)(2,1)} %v_raw.1, s32[1,128]{1,0:T(1,128)} %own_in.1, s32[8,256]{1,0:T(8,128)} %own_l.1, f32[512,512]{1,0:T(8,128)} %omega.1, f32[1,512]{1,0:T(1,128)} %bitcast.9, ...), custom_call_target="tpu_custom_call" | custom-call | tf_op jit(solution)/shard_map/newton/pallas_call | solution.py:583
  133.1 1.3 slice_bitcast_fusion

commit v6 on v5

--- a/solution.py
+++ b/solution.py
@@ -427,7 +427,6 @@
         @pl.when(it > 0)
         def _():
             turn_k()
-            lax.fori_loop(0, 8, take, 0)
             tot[...] = jnp.zeros((512, 256), F32)
             lax.fori_loop(0, 8, blocks, 0)
 
@@ -478,6 +477,7 @@
             out[0] += step * dir_own[...]
             out[1] -= step * (dir_own[...] + t_red[...])
             dir_own[...] = out[1] + beta * dir_own[...]
+            lax.fori_loop(0, 8, take, 0)
 
         @pl.when(it == ITERS - 1)
         def _():

time: 135 us -> 131 us (0.970)
  Pallas kernels: 132 us -> 129 us
    pallas_call x1, Pallas kernels: 132 us -> 129 us  [local(): pl.pallas_call(kernel, out_shape=jax.ShapeDtypeStruct((2, 8, 128), F32),...]
where the time goes in v6:
time: 131 us
  Pallas kernels  129 us (98%)
    pallas_call x1, Pallas kernels, local(): pl.pallas_call(kernel, out_shape=jax.ShapeDtypeStruct((2, 8, 128), F32),...  129 us

profile of v6, /device:TPU:1, one launch (start us, length us, event | category | flops | bytes accessed | tf_op | source)
XLA Modules:
  0.0 131.1 jit_solution(6347237894614215523)
XLA Ops:
  0.6 129.2 %newton.1 = f32[2,8,128]{2,1,0:T(8,128)} custom-call(f32[8,128]{1,0:T(8,128)} %bitcast.8, bf16[96,512]{1,0:T(8,128)(2,1)} %p_own.1, bf16[32,96,128]{2,1,0:T(8,128)(2,1)} %bitcast.7, bf16[128,384]{1,0:T(8,128)(2,1)} %v_raw.1, s32[1,128]{1,0:T(1,128)} %own_in.1, s32[8,256]{1,0:T(8,128)} %own_l.1, f32[512,512]{1,0:T(8,128)} %omega.1, f32[1,512]{1,0:T(1,128)} %bitcast.9, ...), custom_call_target="tpu_custom_call" | custom-call | tf_op jit(solution)/shard_map/newton/pallas_call | solution.py:583
  129.9 1.3 slice_bitcast_fusion
